TPU v7x, 32 devices: a whole 2x2x4 slice. The times are simulated.
32 devices in a mesh: shell: 8 (over z, x), atom: 4 (over y, core).
Axes of the slice: x: 2, y: 2, z: 4, core: 2. Of those that a mesh axis runs over, the one named last changes fastest.
Arguments:
- rho: float32 [32768], P('shell'), may hold values from 0.5 to 1.5
- task_point: int32 [8, 32, 256], P('shell', 'atom'), may hold values from 0 to 4095
- task_count: int32 [8, 32], P('shell', 'atom'), may hold values from 1 to 256
- radial_index: int32 [8, 32, 256], P('shell', 'atom'), may hold values from 0 to 126
- fraction: float32 [8, 32, 256], P('shell', 'atom'), may hold values from 0 to 1
- angular: bfloat16 [8, 32, 49, 256], P('shell', 'atom'), may hold values from -6 to 6
- green: float32 [7, 128, 128], replicated, may hold values from -0.02734375 to 0.02734375
Outputs:
- potential: float32 [32768], P(('shell', 'atom'))
Inputs may be any that keep to these rules, and one draw needn't show every extreme that they name: Slots j with j >= task_count of their atom and batch are unused.
All inputs are finite; a program needn't handle non-finite values.
Results may differ from a plain program's by a relative error of at most 0.005.
Values may be sent and summed in bfloat16 or wider, within the bound.
A program may use at most 64 MiB of HBM per device.

v0:
```python
import math

import jax
import jax.numpy as jnp
import numpy as np
from jax import lax
from jax.sharding import PartitionSpec as P

LM = 49
R = 128


green_width_holder = [R]


def degree_table():
    return np.array([int(math.isqrt(i)) for i in range(LM)], dtype=np.int32)


def radial_rows(radial_index, fraction):
    width = green_width_holder[0]
    grid = jnp.arange(width, dtype=jnp.int32)
    lower = (grid == radial_index[..., None]).astype(jnp.float32) * (1.0 - fraction)[..., None]
    upper = (grid == radial_index[..., None] + 1).astype(jnp.float32) * fraction[..., None]
    return (lower + upper).astype(jnp.bfloat16)


def radial_solve(moments, green):
    kernels = green[degree_table()]
    return jnp.einsum("alq,lqr->alr", moments, kernels, precision=lax.Precision.HIGHEST).astype(
        jnp.bfloat16
    )


def per_device(rho, task_point, task_count, radial_index, fraction, angular, green):
    points = task_point[0]
    counts = task_count[0]
    angles = angular[0]
    slot_ids = jnp.arange(points.shape[1], dtype=jnp.int32)
    live = (slot_ids[None, :] < counts[:, None]).astype(jnp.float32)
    picked = rho[points] * live
    weighted = (angles.astype(jnp.float32) * picked[:, None, :]).astype(jnp.bfloat16)
    rows = radial_rows(radial_index[0], fraction[0])
    partial_value = jnp.einsum("als,asr->alr", weighted, rows, preferred_element_type=jnp.float32)
    moments = lax.psum(partial_value, "shell")
    table = radial_solve(moments, green)
    radial = jnp.einsum("alr,asr->als", table, rows, preferred_element_type=jnp.float32)
    values = jnp.sum(angles.astype(jnp.float32) * radial, axis=1) * live
    terms = jnp.zeros((rho.shape[0],), jnp.float32).at[points.reshape(-1)].add(values.reshape(-1))
    return lax.psum_scatter(terms, "atom", scatter_dimension=0, tiled=True)


def solution(mesh):
    in_specs = (
        P("shell"),
        P("shell", "atom", None),
        P("shell", "atom"),
        P("shell", "atom", None),
        P("shell", "atom", None),
        P("shell", "atom", None, None),
        P(),
    )
    out_specs = P(("shell", "atom"))
    return jax.shard_map(
        per_device, mesh=mesh, in_specs=in_specs, out_specs=out_specs, check_vma=False
    )
```

profile of v0, /device:TPU:0, one launch (start us, length us, event | category | flops | bytes accessed | tf_op | source)
XLA Modules:
  0.0 130.8 jit_solution(7346657215607768732)
XLA Ops:
  6.5 0.0 copy-start
  6.5 0.0 all-reduce.3.cloned.1.call-start
  6.5 0.8 fusion.10
  7.3 0.0 copy-done.1
  7.3 0.0 copy-start.3
  7.3 0.0 copy-start.4
  7.4 0.0 copy-start.5
  7.4 0.0 copy-start.7
  7.4 0.0 copy-start.2
  7.4 0.0 copy-start.6
  7.4 11.8 %gather_fusion.1 = f32[2048]{0:T(1024)S(1)} fusion(f32[4096]{0:T(1024)S(1)} %copy-done.1, s32[2048]{0:T(1024)S(1)} %broadcast_clamp_fusion), kind=kCustom, calls=%fused_computation.1 | custom fusion | bytes 24576 | tf_op jit(solution)/shard_map/gather | solution.py:41
  19.2 0.0 copy-done.3
  19.2 0.0 copy-done.4
  19.2 0.0 copy-done.5
  19.2 0.1 fusion.11
  19.3 0.0 copy-done.7
  19.3 2.7 %fusion.2 = f32[8,49,128]{2,1,0:T(8,128)} fusion(f32[8,256]{1,0:T(8,128)S(1)} %bitcast.36, s32[8,256]{1,0:T(8,128)S(1)} %broadcast_add_fusion, f32[8,256]{1,0:T(8,128)S(1)} %get-tuple-element.6, s32[8,256]{1,0:T(8,128)S(1)} %bitcast.32, f32[8,256]{1,0:T(8,128)S(1)} %get-tuple-element.5, bf16[1,8,49,256]{3,1,2,0:T(8,128)(2,1)S(1)} %copy-done.7), kind=kOutput, calls=%fused_computation.11 | convolution fusion | flops 27564032 | bytes 442368 | tf_op jit(solution)/shard_map/als,asr->alr/dot_general | solution.py:44
  22.0 0.0 all-reduce.3.cloned.1.call-update
  22.0 0.0 copy-done.2
  22.1 0.0 copy-done.6
  22.1 0.0 copy-done
  22.1 0.0 copy-start.8
  22.1 2.4 %gather_fusion = f32[49,128,128]{2,1,0:T(8,128)} fusion(f32[7,128,128]{2,1,0:T(8,128)S(1)} %copy-done, s32[1024]{0:T(1024)S(1)} %pad_clamp_fusion), kind=kCustom, calls=%fused_computation | custom fusion | bytes 6422724 | tf_op jit(solution)/shard_map/gather | solution.py:29
  24.5 0.0 copy-done.8
  24.5 0.6 dynamic-slice
  25.8 69.5 %all-reduce.3.cloned.1.call-done = f32[8,49,128]{2,1,0:T(8,128)} async-done(((f32[8,49,128]{2,1,0:T(8,128)}), f32[8,49,128]{2,1,0:T(8,128)}) %all-reduce.3.cloned.1.call-update) | async-done | bytes 200720 | tf_op jit(solution)/shard_map/psum | solution.py:45
  95.2 4.7 %fusion.1 = bf16[8,49,128]{2,0,1:T(8,128)(2,1)S(1)} fusion(f32[49,128,128]{2,1,0:T(8,128)} %gather_fusion, f32[8,49,128]{2,1,0:T(8,128)} %all-reduce.3.cloned.1.call-done), kind=kOutput, calls=%fused_computation.6 | convolution fusion | flops 77120512 | bytes 3512320 | tf_op jit(solution)/shard_map/alq,lqr->alr/dot_general | solution.py:30
  100.0 1.9 %fusion = f32[8,256]{1,0:T(8,128)S(1)} fusion(f32[8,256]{1,0:T(8,128)S(1)} %bitcast.37, s32[8,256]{1,0:T(8,128)S(1)} %broadcast_add_fusion, f32[8,256]{1,0:T(8,128)S(1)} %get-tuple-element.6, s32[8,256]{1,0:T(8,128)S(1)} %bitcast.33, bf16[1,8,49,256]{3,1,2,0:T(8,128)(2,1)S(1)} %copy-done.7, bf16[8,49,128]{2,0,1:T(8,128)(2,1)S(1)} %fusion.1), kind=kOutput, calls=%fused_computation.4 | convolution fusion | flops 27561984 | bytes 342016 | tf_op jit(solution)/shard_map/alr,asr->als/dot_general | solution.py:47
  101.9 0.1 select_bitcast_fusion
  102.0 11.2 %scatter_custom_fusion = f32[4096]{0:T(1024)S(1)} fusion(s32[2048]{0:T(1024)S(1)} %bitcast.34, f32[2048]{0:T(1024)S(1)} %bitcast.35, f32[]{:T(128)} %constant.8.clone.1), kind=kCustom, calls=%fused_computation.24 | custom fusion | flops 2048 | bytes 16388 | tf_op jit(solution)/shard_map/scatter-add | solution.py:49
  113.3 10.1 %all-reduce = f32[4096]{0:T(1024)S(1)} all-reduce(f32[4096]{0:T(1024)S(1)} %scatter_custom_fusion), channel_id=2, replica_groups=mesh['shell'=8,'atom'=4] {'atom'}, use_global_device_ids=true, to_apply=%region_3.0.clone | all-reduce | flops 4096 | bytes 32768
  123.4 0.6 dynamic-slice.1
  (9 shorter events, 0.1 us)
Async XLA Ops:
  6.5 15.5 %copy-start = (f32[7,128,128]{2,1,0:T(8,128)S(1)}, f32[7,128,128]{2,1,0:T(8,128)}, u32[]{:S(2)}) copy-start(f32[7,128,128]{2,1,0:T(8,128)} %param.15) | copy-start | bytes 1376260
  6.5 0.8 copy-start.1
  6.5 88.7 %all-reduce.3.cloned.1.call-start = ((), (), s32[]{:S(2)}) async-start(), calls=%async_computation | async-start | bytes 458752 | tf_op jit(solution)/shard_map/psum | solution.py:45
  7.3 11.9 %copy-start.3 = (s32[1,8,256]{2,1,0:T(8,128)S(1)}, s32[1,8,256]{2,1,0:T(8,128)}, u32[]{:S(2)}) copy-start(s32[1,8,256]{2,1,0:T(8,128)} %param.12) | copy-start | bytes 24580
  7.3 11.9 %copy-start.4 = (f32[1,8,256]{2,1,0:T(8,128)S(1)}, f32[1,8,256]{2,1,0:T(8,128)}, u32[]{:S(2)}) copy-start(f32[1,8,256]{2,1,0:T(8,128)} %param.13) | copy-start | bytes 24580
  7.4 11.9 %copy-start.5 = (s32[1,8]{1,0:T(1,128)S(1)}, s32[1,8]{1,0:T(1,128)}, u32[]{:S(2)}) copy-start(s32[1,8]{1,0:T(1,128)} %param.11) | copy-start | bytes 100
  7.4 12.0 %copy-start.7 = (bf16[1,8,49,256]{3,1,2,0:T(8,128)(2,1)S(1)}, bf16[1,8,49,256]{3,1,2,0:T(8,128)(2,1)}, u32[]{:S(2)}) copy-start(bf16[1,8,49,256]{3,1,2,0:T(8,128)(2,1)} %param.14) | copy-start | bytes 602116
  7.4 14.6 %copy-start.2 = (s32[1,8,256]{2,1,0:T(8,128)S(1)}, s32[1,8,256]{2,1,0:T(8,128)}, u32[]{:S(2)}) copy-start(s32[1,8,256]{2,1,0:T(8,128)} %param.10) | copy-start | bytes 24580
  7.4 14.7 %copy-start.6 = (s32[49]{0:T(128)S(1)}, s32[49]{0:T(128)}, u32[]{:S(2)}) copy-start(s32[49]{0:T(128)} %constant.31) | copy-start | bytes 592
  22.1 2.4 %copy-start.8 = (u32[32]{0:T(128)S(1)}, u32[32]{0:T(128)}, u32[]{:S(2)}) copy-start(u32[32]{0:T(128)} %constant.34) | copy-start | bytes 388
Sparse Core Ops, SparseCore 0:
  22.1 73.0 all-reduce.2
where the time goes:
time: 131 us
  waiting for transfers between devices  69.5 us (53%)
  local copies, waits for them, and re-layouts  15.5 us (12%)
  between operations  14.2 us (11%)
  other arithmetic  12.2 us (9%)
  blocking collectives  10.1 us (8%)
  matrix products  9.32 us (7%)
    psum x1, waiting for transfers between devices, per_device(): moments = lax.psum(partial_value, 'shell')  69.5 us
    gather x2, local copies, waits for them, and re-layouts, per_device(): picked = rho[points] * live  11.8 us
    scatter-add x1, other arithmetic, per_device(): jnp.zeros((rho.shape[0],), jnp.float32).at[points.reshape(-1)]  11.2 us
    unnamed x1, blocking collectives  10.1 us
    dot_general x1, matrix products, radial_solve(): jnp.einsum('alq,lqr->alr', moments, kernels, precision=lax.Precision.HIGH...  4.72 us
    dot_general x1, matrix products, per_device(): jnp.einsum('als,asr->alr', weighted, rows, preferred_element_type=jnp.flo...  2.65 us
  transfers between devices with their start and end apart: 1, of which 1 were waited for; matrix products, arithmetic and copies ran while one was open for 2% of the time, Pallas kernels for 0%

commit v1 on v0

v1 whole, which is shorter than its diff:
```python
import functools
import math

import jax
import jax.numpy as jnp
from jax import lax
from jax.experimental import pallas as pl
from jax.experimental.pallas import tpu as pltpu
from jax.sharding import PartitionSpec as P

MESH = pl.DeviceIdType.MESH
LANES = 128
NT = (((1,), (1,)), ((), ()))


def repeat(count, body):
    if count <= 16:
        for i in range(count):
            body(i)
    else:
        lax.fori_loop(0, count, lambda i, c: (body(i), c)[1], 0)


def split2(x):
    high = x.astype(jnp.bfloat16)
    low = (x - high.astype(jnp.float32)).astype(jnp.bfloat16)
    return high, low


def kernel(n_shell, n_atom, rho_h, pts_h, cnt_h, idx_h, frac_h, ang_h, green_h, out_ref,
           rho_v, pts_v, cnt_v, idx_v, frac_v, ang_v, green_v,
           live_v, low_v, high_v, onehot, meta_v, rmeta, rang, rows_v, gh_v, gl_v,
           moments, val_v, rval, part_v, rpart,
           local_sem, s_ang, r_ang, s_meta, r_meta, s_val, r_val, s_part, r_part):
    me, ma = lax.axis_index("shell"), lax.axis_index("atom")
    atoms, lm, slots = ang_v.shape
    lmp = rang.shape[1]
    body_rows = (lm // 16) * 16
    rest = lm - body_rows
    degrees, width = green_v.shape[0], green_v.shape[1]
    coarse = rho_v.shape[0]

    def load(i, src, dst):
        copy = pltpu.make_async_copy(src, dst, local_sem.at[i])
        copy.start()
        return copy

    c_ang = load(0, ang_h.at[0], ang_v)
    c_pts = load(1, pts_h.at[0], pts_v)
    c_rho = load(2, rho_h, rho_v)
    c_idx = load(3, idx_h.at[0], idx_v)
    c_cnt = load(4, cnt_h, cnt_v)
    c_frac = load(5, frac_h.at[0], frac_v)
    c_green = load(6, green_h, green_v)

    def shell_at(k):
        return lax.rem(me + k, n_shell)

    def atom_at(k):
        return lax.rem(ma + k, n_atom)

    def far_first(i):
        half = n_shell // 2
        step = (i + 1) // 2
        return half + step * (1 - 2 * (i % 2))

    barrier = pltpu.get_barrier_semaphore()
    repeat(n_shell - 1, lambda i: pl.semaphore_signal(
        barrier, inc=1, device_id=(shell_at(i + 1), ma), device_id_type=MESH))
    repeat(n_atom - 1, lambda i: pl.semaphore_signal(
        barrier, inc=1, device_id=(me, atom_at(i + 1)), device_id_type=MESH))
    pl.semaphore_wait(barrier, n_shell + n_atom - 2)

    def ang_copy(to, slot):
        return pltpu.make_async_remote_copy(
            src_ref=ang_v.at[to, pl.ds(0, body_rows)], dst_ref=rang.at[slot, pl.ds(0, body_rows)],
            send_sem=s_ang.at[to], recv_sem=r_ang.at[slot],
            device_id=(to, ma), device_id_type=MESH)

    def meta_copy(to, slot):
        return pltpu.make_async_remote_copy(
            src_ref=meta_v.at[to], dst_ref=rmeta.at[slot],
            send_sem=s_meta.at[to], recv_sem=r_meta.at[slot],
            device_id=(to, ma), device_id_type=MESH)

    def val_copy(to, slot):
        return pltpu.make_async_remote_copy(
            src_ref=val_v.at[to], dst_ref=rval.at[slot],
            send_sem=s_val.at[to], recv_sem=r_val.at[slot],
            device_id=(to, ma), device_id_type=MESH)

    def part_copy(to, slot):
        return pltpu.make_async_remote_copy(
            src_ref=part_v.at[to], dst_ref=rpart.at[slot],
            send_sem=s_part.at[to], recv_sem=r_part.at[slot],
            device_id=(me, to), device_id_type=MESH)

    c_ang.wait()

    def send_ang(i):
        ang_copy(shell_at(far_first(i)), me).start()

    repeat(n_shell - 1, send_ang)
    rang[me, 0:body_rows] = ang_v[me, 0:body_rows]

    c_pts.wait()
    c_rho.wait()
    c_idx.wait()
    c_cnt.wait()
    c_frac.wait()
    low_v[...] = pts_v[...] & (LANES - 1)
    high_v[...] = pts_v[...] >> (LANES.bit_length() - 1)
    count_row = jnp.broadcast_to(cnt_v[...].astype(jnp.float32), (atoms, atoms))
    diagonal = (lax.broadcasted_iota(jnp.int32, (atoms, atoms), 0)
                == lax.broadcasted_iota(jnp.int32, (atoms, atoms), 1))
    counts = jnp.sum(jnp.where(diagonal, count_row, 0.0), axis=1, keepdims=True)
    slot_ids = lax.broadcasted_iota(jnp.int32, (atoms, slots), 1).astype(jnp.float32)
    live_v[...] = jnp.where(slot_ids < counts, idx_v[...].astype(jnp.float32), -8.0)

    rho = rho_v[...]
    rho_1, left = rho.astype(jnp.bfloat16), rho
    left = left - rho_1.astype(jnp.float32)
    rho_2, rho_3 = split2(left)
    rho_parts = jnp.concatenate(
        [rho_1.astype(jnp.float32), rho_2.astype(jnp.float32), rho_3.astype(jnp.float32)],
        axis=0).astype(jnp.bfloat16)
    fine_ids = lax.broadcasted_iota(jnp.int32, (LANES, slots), 0)
    coarse_ids = lax.broadcasted_iota(jnp.int32, (coarse, slots), 0)

    def build_meta(a):
        hot = jnp.where(fine_ids == low_v[pl.ds(a, 1), :], 1.0, 0.0).astype(jnp.bfloat16)
        onehot[a] = hot
        found = jnp.dot(rho_parts, hot, preferred_element_type=jnp.float32)
        found = found[0:coarse] + found[coarse:2 * coarse] + found[2 * coarse:3 * coarse]
        here = coarse_ids == high_v[pl.ds(a, 1), :]
        meta_v[a, 0:1, :] = jnp.sum(jnp.where(here, found, 0.0), axis=0, keepdims=True)
        meta_v[a, 1:2, :] = live_v[pl.ds(a, 1), :]
        meta_v[a, 2:3, :] = frac_v[pl.ds(a, 1), :]
        for j in range(rest):
            meta_v[a, 3 + j:4 + j, :] = ang_v[a, body_rows + j:body_rows + j + 1, :].astype(jnp.float32)

    def send_meta(i):
        to = shell_at(far_first(i))
        build_meta(to)
        meta_copy(to, me).start()

    repeat(n_shell - 1, send_meta)
    build_meta(me)
    rmeta[me] = meta_v[me]

    c_green.wait()
    green = green_v[...].reshape(degrees * width, width)
    gh, gl = split2(green)
    gh_v[...] = gh
    gl_v[...] = gl

    moments[...] = jnp.zeros_like(moments)
    grid_ids = lax.broadcasted_iota(jnp.int32, (width, slots), 0).astype(jnp.float32)
    tail_ids = lax.broadcasted_iota(jnp.int32, (lmp - body_rows, slots), 0)

    def add_batch(s):
        index, fraction = rmeta[s, 1:2, :], rmeta[s, 2:3, :]
        offset = grid_ids - index
        rows = jnp.where(offset == 0.0, 1.0 - fraction, jnp.where(offset == 1.0, fraction, 0.0))
        rows = rows.astype(jnp.bfloat16)
        rows_v[s] = rows
        tail = jnp.zeros((lmp - body_rows, slots), jnp.float32)
        for j in range(rest):
            tail = jnp.where(tail_ids == j, rmeta[s, 3 + j:4 + j, :], tail)
        rang[s, body_rows:lmp] = tail.astype(jnp.bfloat16)
        weighted = (rang[s].astype(jnp.float32) * rmeta[s, 0:1, :]).astype(jnp.bfloat16)
        moments[...] += lax.dot_general(weighted, rows, NT, preferred_element_type=jnp.float32)

    def take_batch(i):
        s = lax.rem(me + n_shell - far_first(n_shell - 2 - i), n_shell)
        ang_copy(me, s).wait_recv()
        meta_copy(me, s).wait_recv()
        add_batch(s)

    add_batch(me)
    repeat(n_shell - 1, take_batch)

    mom = moments[...]
    mom_h, mom_l = split2(mom)
    both = jnp.concatenate([mom_h.astype(jnp.float32), mom_l.astype(jnp.float32)], axis=0)
    row_ids = lax.broadcasted_iota(jnp.int32, (2 * lmp, width), 0)
    row_ids = jnp.where(row_ids >= lmp, row_ids - lmp, row_ids)
    spread = jnp.concatenate(
        [jnp.where((row_ids >= l * l) & (row_ids < (l + 1) * (l + 1)), both, 0.0)
         for l in range(degrees)], axis=1).astype(jnp.bfloat16)
    first = jnp.dot(spread, gh_v[...], preferred_element_type=jnp.float32)
    second = jnp.dot(spread[0:lmp], gl_v[...], preferred_element_type=jnp.float32)
    table = (first[0:lmp] + first[lmp:] + second).astype(jnp.bfloat16)

    def evaluate(b, out, at):
        radial = jnp.dot(table, rows_v[b], preferred_element_type=jnp.float32)
        out[at] = jnp.sum(rang[b].astype(jnp.float32) * radial, axis=0, keepdims=True)

    def send_val(i):
        to = shell_at(far_first(i))
        evaluate(to, val_v, to)
        val_copy(to, me).start()

    repeat(n_shell - 1, send_val)
    evaluate(me, rval, me)

    def placed(a):
        spot = jnp.where(coarse_ids == high_v[pl.ds(a, 1), :], rval[a], 0.0)
        spot_h, spot_l = split2(spot)
        spots = jnp.concatenate(
            [spot_h.astype(jnp.float32), spot_l.astype(jnp.float32)], axis=0).astype(jnp.bfloat16)
        return lax.dot_general(spots, onehot[a], NT, preferred_element_type=jnp.float32)

    def terms_of(i, terms):
        s = lax.rem(me + n_shell - far_first(n_shell - 2 - i), n_shell)
        val_copy(me, s).wait_recv()
        return terms + placed(s)

    terms = placed(me)
    if n_shell <= 16:
        for i in range(n_shell - 1):
            terms = terms_of(i, terms)
    else:
        terms = lax.fori_loop(0, n_shell - 1, terms_of, terms)
    terms = terms[0:coarse] + terms[coarse:]
    share = coarse // n_atom
    for g in range(n_atom):
        part_v[g] = terms[g * share:(g + 1) * share]

    repeat(n_atom - 1, lambda i: part_copy(atom_at(i + 1), ma).start())
    rpart[ma] = part_v[ma]

    def take_part(i):
        part_copy(ma, atom_at(i + 1)).wait_recv()

    repeat(n_atom - 1, take_part)
    total = rpart[0]
    for g in range(1, n_atom):
        total = total + rpart[g]
    out_ref[...] = total

    def finish(i):
        to = shell_at(i + 1)
        ang_copy(to, me).wait_send()
        meta_copy(to, me).wait_send()
        val_copy(to, me).wait_send()

    repeat(n_shell - 1, finish)
    repeat(n_atom - 1, lambda i: part_copy(atom_at(i + 1), ma).wait_send())


def solution(mesh):
    n_shell, n_atom = mesh.shape["shell"], mesh.shape["atom"]

    def per_device(rho, task_point, task_count, radial_index, fraction, angular, green):
        _, atoms, lm, slots = angular.shape
        points = rho.shape[0]
        degrees, width, _ = green.shape
        assert atoms == n_shell and points % (LANES * n_atom) == 0
        assert degrees == math.isqrt(lm)
        coarse = points // LANES
        share = coarse // n_atom
        lmp = (lm // 16 + 1) * 16
        meta_rows = 3 + lm % 16
        f32, bf16, i32 = jnp.float32, jnp.bfloat16, jnp.int32
        vmem = pltpu.VMEM
        scratch = [
            vmem((coarse, LANES), f32),
            vmem((atoms, slots), i32),
            vmem((1, atoms), i32),
            vmem((atoms, slots), i32),
            vmem((atoms, slots), f32),
            vmem((atoms, lm, slots), bf16),
            vmem((degrees, width, width), f32),
            vmem((atoms, slots), f32),
            vmem((atoms, slots), i32),
            vmem((atoms, slots), i32),
            vmem((atoms, LANES, slots), bf16),
            vmem((atoms, meta_rows, slots), f32),
            vmem((n_shell, meta_rows, slots), f32),
            vmem((n_shell, lmp, slots), bf16),
            vmem((n_shell, width, slots), bf16),
            vmem((degrees * width, width), bf16),
            vmem((degrees * width, width), bf16),
            vmem((lmp, width), f32),
            vmem((n_shell, 1, slots), f32),
            vmem((n_shell, 1, slots), f32),
            vmem((n_atom, share, LANES), f32),
            vmem((n_atom, share, LANES), f32),
            pltpu.SemaphoreType.DMA((7,)),
        ] + [pltpu.SemaphoreType.DMA((n_shell,))] * 6 + [pltpu.SemaphoreType.DMA((n_atom,))] * 2
        out = pl.pallas_call(
            functools.partial(kernel, n_shell, n_atom),
            out_shape=jax.ShapeDtypeStruct((share, LANES), f32),
            in_specs=[pl.BlockSpec(memory_space=pl.ANY)] * 7,
            out_specs=pl.BlockSpec(memory_space=pltpu.VMEM),
            scratch_shapes=scratch,
            compiler_params=pltpu.CompilerParams(
                collective_id=0, has_side_effects=True, vmem_limit_bytes=48 * 1024 * 1024),
            name="hartree",
        )(rho.reshape(coarse, LANES), task_point, task_count, radial_index, fraction, angular, green)
        return out.reshape(share * LANES)

    in_specs = (
        P("shell"),
        P("shell", "atom", None),
        P("shell", "atom"),
        P("shell", "atom", None),
        P("shell", "atom", None),
        P("shell", "atom", None, None),
        P(),
    )
    return jax.shard_map(
        per_device, mesh=mesh, in_specs=in_specs, out_specs=P(("shell", "atom")), check_vma=False
    )
```

time: 131 us -> 25.7 us (0.20)
  waiting for transfers between devices: 69.5 us -> 0 us
  Pallas kernels: 0 us -> 22.8 us
  between operations: 14.2 us -> 0.07 us
  local copies, waits for them, and re-layouts: 15.5 us -> 2.66 us
  other arithmetic: 12.2 us -> 0 us
  blocking collectives: 10.1 us -> 0 us
  matrix products: 9.32 us -> 0 us
    psum x1 -> x0, waiting for transfers between devices: 69.5 us -> none  [per_device(): moments = lax.psum(partial_value, 'shell')]
    pallas_call x0 -> x1, Pallas kernels: none -> 22.8 us  [per_device(): pl.pallas_call(functools.partial(kernel, n_shell, n_atom), out_shape=jax....]
    gather x3 -> x0, local copies, waits for them, and re-layouts: 14.2 us -> none  [the longest x2 11.8 us: per_device(): picked = rho[points] * live]
    scatter-add x1 -> x0, other arithmetic: 11.2 us -> none  [per_device(): jnp.zeros((rho.shape[0],), jnp.float32).at[points.reshape(-1)]]
    unnamed x1 -> x0, blocking collectives: 10.1 us -> none
    dot_general x3 -> x0, matrix products: 9.32 us -> none  [the longest x1 4.72 us: radial_solve(): jnp.einsum('alq,lqr->alr', moments, kernels, precision=lax.Precision.HIGH...]
    unnamed x23 -> x14, local copies, waits for them, and re-layouts: 1.26 us -> 2.66 us
  transfers between devices with their start and end apart: 1 -> 0, of which waited for: 1 -> 0; matrix products, arithmetic and copies ran while one was open for 2% -> 0% of each run, Pallas kernels for 0% -> 0%
where the time goes in v1:
time: 25.7 us; the launch traced here: 25.5 us
  Pallas kernels  22.8 us (89%)
  local copies, waits for them, and re-layouts  2.66 us (10%)
    pallas_call x1, Pallas kernels, per_device(): pl.pallas_call(functools.partial(kernel, n_shell, n_atom), out_shape=jax....  22.8 us
    unnamed x14, local copies, waits for them, and re-layouts  2.66 us

profile of v1, /device:TPU:0, one launch (start us, length us, event | category | flops | bytes accessed | tf_op | source)
XLA Modules:
  0.0 25.5 jit_solution(16411972136346479284)
XLA Ops:
  0.0 0.0 copy-start.1
  0.0 0.0 copy-start.2
  0.0 0.0 copy-start.3
  0.0 0.0 copy-start.4
  0.0 0.0 copy-start.5
  0.0 1.0 %copy.8.ang_h = bf16[1,8,49,256]{3,2,1,0:T(8,128)(2,1)S(1)} copy(bf16[1,8,49,256]{3,1,2,0:T(8,128)(2,1)} %param.12) | data formatting | bytes 401408 | tf_op args[5]
  1.1 0.0 copy-done.1
  1.1 0.0 copy-done.2
  1.1 0.0 copy-done.3
  1.1 0.0 copy-done.4
  1.1 0.0 copy-done.5
  1.1 0.0 copy-start
  1.1 1.0 %copy-done = f32[7,128,128]{2,1,0:T(8,128)S(1)} copy-done((f32[7,128,128]{2,1,0:T(8,128)S(1)}, f32[7,128,128]{2,1,0:T(8,128)}, u32[]{:S(2)}) %copy-start) | copy-done | bytes 458776
  2.1 22.8 %hartree.1 = f32[8,128]{1,0:T(8,128)S(1)} custom-call(f32[32,128]{1,0:T(8,128)S(1)} %bitcast.3, s32[1,8,256]{2,1,0:T(8,128)S(1)} %copy-done.2, s32[1,8]{1,0:T(1,128)S(1)} %copy-done.5, s32[1,8,256]{2,1,0:T(8,128)S(1)} %copy-done.3, f32[1,8,256]{2,1,0:T(8,128)S(1)} %copy-done.4, bf16[1,8,49,256]{3,2,1,0:T(8,128)(2,1)S(1)} %copy.8.ang_h, ...), custom_call_target="tpu_custom_call" | custom-call | tf_op jit(solution)/shard_map/hartree/pallas_call | solution.py:292
  24.9 0.6 %copy.10 = f32[1024]{0:T(1024)} copy(f32[1024]{0:T(1024)S(1)} %bitcast.2) | data formatting | bytes 8192
Async XLA Ops:
  0.0 1.1 %copy-start.1 = (f32[4096]{0:T(1024)S(1)}, f32[4096]{0:T(1024)}, u32[]{:S(2)}) copy-start(f32[4096]{0:T(1024)} %param.7) | copy-start | bytes 49156
  0.0 1.1 %copy-start.2 = (s32[1,8,256]{2,1,0:T(8,128)S(1)}, s32[1,8,256]{2,1,0:T(8,128)}, u32[]{:S(2)}) copy-start(s32[1,8,256]{2,1,0:T(8,128)} %pts_h.1) | copy-start | bytes 24580
  0.0 1.1 %copy-start.3 = (s32[1,8,256]{2,1,0:T(8,128)S(1)}, s32[1,8,256]{2,1,0:T(8,128)}, u32[]{:S(2)}) copy-start(s32[1,8,256]{2,1,0:T(8,128)} %idx_h.1) | copy-start | bytes 24580
  0.0 1.1 %copy-start.4 = (f32[1,8,256]{2,1,0:T(8,128)S(1)}, f32[1,8,256]{2,1,0:T(8,128)}, u32[]{:S(2)}) copy-start(f32[1,8,256]{2,1,0:T(8,128)} %frac_h.1) | copy-start | bytes 24580
  0.0 1.1 %copy-start.5 = (s32[1,8]{1,0:T(1,128)S(1)}, s32[1,8]{1,0:T(1,128)}, u32[]{:S(2)}) copy-start(s32[1,8]{1,0:T(1,128)} %cnt_h.1) | copy-start | bytes 100
  1.1 1.0 %copy-start = (f32[7,128,128]{2,1,0:T(8,128)S(1)}, f32[7,128,128]{2,1,0:T(8,128)}, u32[]{:S(2)}) copy-start(f32[7,128,128]{2,1,0:T(8,128)} %green_h.1) | copy-start | bytes 1376260

commit v2 on v1

--- a/solution.py
+++ b/solution.py
@@ -21,6 +21,14 @@
         lax.fori_loop(0, count, lambda i, c: (body(i), c)[1], 0)
 
 
+def accumulate(count, body, total):
+    if count <= 16:
+        for i in range(count):
+            total = total + body(i)
+        return total
+    return lax.fori_loop(0, count, lambda i, c: c + body(i), total)
+
+
 def split2(x):
     high = x.astype(jnp.bfloat16)
     low = (x - high.astype(jnp.float32)).astype(jnp.bfloat16)
@@ -28,15 +36,16 @@
 
 
 def kernel(n_shell, n_atom, rho_h, pts_h, cnt_h, idx_h, frac_h, ang_h, green_h, out_ref,
-           rho_v, pts_v, cnt_v, idx_v, frac_v, ang_v, green_v,
+           rho_v, pts_v, cnt_v, idx_v, frac_v, ang_s, ang_f, ang_v, green_v,
            live_v, low_v, high_v, onehot, meta_v, rmeta, rang, rows_v, gh_v, gl_v,
-           moments, val_v, rval, part_v, rpart,
+           val_v, rval, part_v, rpart,
            local_sem, s_ang, r_ang, s_meta, r_meta, s_val, r_val, s_part, r_part):
     me, ma = lax.axis_index("shell"), lax.axis_index("atom")
-    atoms, lm, slots = ang_v.shape
+    lm, atoms, slots = ang_s.shape
     lmp = rang.shape[1]
-    body_rows = (lm // 16) * 16
+    body_rows = ang_v.shape[1]
     rest = lm - body_rows
+    halves = slots // LANES
     degrees, width = green_v.shape[0], green_v.shape[1]
     coarse = rho_v.shape[0]
 
@@ -45,7 +54,7 @@
         copy.start()
         return copy
 
-    c_ang = load(0, ang_h.at[0], ang_v)
+    c_ang = load(0, ang_h.at[0], ang_s)
     c_pts = load(1, pts_h.at[0], pts_v)
     c_rho = load(2, rho_h, rho_v)
     c_idx = load(3, idx_h.at[0], idx_v)
@@ -69,11 +78,10 @@
         barrier, inc=1, device_id=(shell_at(i + 1), ma), device_id_type=MESH))
     repeat(n_atom - 1, lambda i: pl.semaphore_signal(
         barrier, inc=1, device_id=(me, atom_at(i + 1)), device_id_type=MESH))
-    pl.semaphore_wait(barrier, n_shell + n_atom - 2)
 
     def ang_copy(to, slot):
         return pltpu.make_async_remote_copy(
-            src_ref=ang_v.at[to, pl.ds(0, body_rows)], dst_ref=rang.at[slot, pl.ds(0, body_rows)],
+            src_ref=ang_v.at[to], dst_ref=rang.at[slot, pl.ds(0, body_rows)],
             send_sem=s_ang.at[to], recv_sem=r_ang.at[slot],
             device_id=(to, ma), device_id_type=MESH)
 
@@ -97,11 +105,25 @@
 
     c_ang.wait()
 
-    def send_ang(i):
-        ang_copy(shell_at(far_first(i)), me).start()
-
-    repeat(n_shell - 1, send_ang)
-    rang[me, 0:body_rows] = ang_v[me, 0:body_rows]
+    def widen(m):
+        at = pl.multiple_of(m * atoms, 8) if atoms % 8 == 0 else m * atoms
+        for h in range(halves):
+            ang_f[h, pl.ds(at, atoms), :] = ang_s[m, :, h * LANES:(h + 1) * LANES].astype(jnp.float32)
+
+    def by_atom(a):
+        for h in range(halves):
+            ang_v[a, :, h * LANES:(h + 1) * LANES] = ang_f[
+                h, pl.ds(a, body_rows, stride=atoms), :].astype(jnp.bfloat16)
+
+    if atoms <= 16:
+        for m in range(lm):
+            widen(m)
+    else:
+        repeat(lm, widen)
+    repeat(atoms, by_atom)
+    pl.semaphore_wait(barrier, n_shell + n_atom - 2)
+    repeat(n_shell - 1, lambda i: ang_copy(shell_at(far_first(i)), me).start())
+    rang[me, 0:body_rows] = ang_v[me]
 
     c_pts.wait()
     c_rho.wait()
@@ -137,15 +159,12 @@
         meta_v[a, 1:2, :] = live_v[pl.ds(a, 1), :]
         meta_v[a, 2:3, :] = frac_v[pl.ds(a, 1), :]
         for j in range(rest):
-            meta_v[a, 3 + j:4 + j, :] = ang_v[a, body_rows + j:body_rows + j + 1, :].astype(jnp.float32)
-
-    def send_meta(i):
-        to = shell_at(far_first(i))
-        build_meta(to)
-        meta_copy(to, me).start()
-
-    repeat(n_shell - 1, send_meta)
-    build_meta(me)
+            for h in range(halves):
+                meta_v[a, 3 + j:4 + j, h * LANES:(h + 1) * LANES] = ang_f[
+                    h, pl.ds((body_rows + j) * atoms + a, 1), :]
+
+    repeat(atoms, build_meta)
+    repeat(n_shell - 1, lambda i: meta_copy(shell_at(far_first(i)), me).start())
     rmeta[me] = meta_v[me]
 
     c_green.wait()
@@ -154,7 +173,6 @@
     gh_v[...] = gh
     gl_v[...] = gl
 
-    moments[...] = jnp.zeros_like(moments)
     grid_ids = lax.broadcasted_iota(jnp.int32, (width, slots), 0).astype(jnp.float32)
     tail_ids = lax.broadcasted_iota(jnp.int32, (lmp - body_rows, slots), 0)
 
@@ -169,18 +187,16 @@
             tail = jnp.where(tail_ids == j, rmeta[s, 3 + j:4 + j, :], tail)
         rang[s, body_rows:lmp] = tail.astype(jnp.bfloat16)
         weighted = (rang[s].astype(jnp.float32) * rmeta[s, 0:1, :]).astype(jnp.bfloat16)
-        moments[...] += lax.dot_general(weighted, rows, NT, preferred_element_type=jnp.float32)
+        return lax.dot_general(weighted, rows, NT, preferred_element_type=jnp.float32)
 
     def take_batch(i):
         s = lax.rem(me + n_shell - far_first(n_shell - 2 - i), n_shell)
         ang_copy(me, s).wait_recv()
         meta_copy(me, s).wait_recv()
-        add_batch(s)
-
-    add_batch(me)
-    repeat(n_shell - 1, take_batch)
-
-    mom = moments[...]
+        return add_batch(s)
+
+    mom = accumulate(n_shell - 1, take_batch, add_batch(me))
+
     mom_h, mom_l = split2(mom)
     both = jnp.concatenate([mom_h.astype(jnp.float32), mom_l.astype(jnp.float32)], axis=0)
     row_ids = lax.broadcasted_iota(jnp.int32, (2 * lmp, width), 0)
@@ -196,12 +212,14 @@
         radial = jnp.dot(table, rows_v[b], preferred_element_type=jnp.float32)
         out[at] = jnp.sum(rang[b].astype(jnp.float32) * radial, axis=0, keepdims=True)
 
-    def send_val(i):
+    def evaluate_to(i):
         to = shell_at(far_first(i))
         evaluate(to, val_v, to)
-        val_copy(to, me).start()
-
-    repeat(n_shell - 1, send_val)
+
+    first_part = n_shell // 2
+    for low, high in ((0, first_part), (first_part, n_shell - 1)):
+        repeat(high - low, lambda i: evaluate_to(i + low))
+        repeat(high - low, lambda i: val_copy(shell_at(far_first(i + low)), me).start())
     evaluate(me, rval, me)
 
     def placed(a):
@@ -211,17 +229,8 @@
             [spot_h.astype(jnp.float32), spot_l.astype(jnp.float32)], axis=0).astype(jnp.bfloat16)
         return lax.dot_general(spots, onehot[a], NT, preferred_element_type=jnp.float32)
 
-    def terms_of(i, terms):
-        s = lax.rem(me + n_shell - far_first(n_shell - 2 - i), n_shell)
-        val_copy(me, s).wait_recv()
-        return terms + placed(s)
-
-    terms = placed(me)
-    if n_shell <= 16:
-        for i in range(n_shell - 1):
-            terms = terms_of(i, terms)
-    else:
-        terms = lax.fori_loop(0, n_shell - 1, terms_of, terms)
+    repeat(n_shell - 1, lambda i: val_copy(me, shell_at(i + 1)).wait_recv())
+    terms = accumulate(n_shell - 1, lambda i: placed(i + 1), placed(0))
     terms = terms[0:coarse] + terms[coarse:]
     share = coarse // n_atom
     for g in range(n_atom):
@@ -270,7 +279,9 @@
             vmem((1, atoms), i32),
             vmem((atoms, slots), i32),
             vmem((atoms, slots), f32),
-            vmem((atoms, lm, slots), bf16),
+            vmem((lm, atoms, slots), bf16),
+            vmem((slots // LANES, lm * atoms, LANES), f32),
+            vmem((atoms, lm // 16 * 16, slots), bf16),
             vmem((degrees, width, width), f32),
             vmem((atoms, slots), f32),
             vmem((atoms, slots), i32),
@@ -282,7 +293,6 @@
             vmem((n_shell, width, slots), bf16),
             vmem((degrees * width, width), bf16),
             vmem((degrees * width, width), bf16),
-            vmem((lmp, width), f32),
             vmem((n_shell, 1, slots), f32),
             vmem((n_shell, 1, slots), f32),
             vmem((n_atom, share, LANES), f32),
@@ -292,13 +302,14 @@
         out = pl.pallas_call(
             functools.partial(kernel, n_shell, n_atom),
             out_shape=jax.ShapeDtypeStruct((share, LANES), f32),
-            in_specs=[pl.BlockSpec(memory_space=pl.ANY)] * 7,
+            in_specs=[pl.BlockSpec(memory_space=pltpu.HBM)] * 7,
             out_specs=pl.BlockSpec(memory_space=pltpu.VMEM),
             scratch_shapes=scratch,
             compiler_params=pltpu.CompilerParams(
-                collective_id=0, has_side_effects=True, vmem_limit_bytes=48 * 1024 * 1024),
+                collective_id=0, has_side_effects=True, vmem_limit_bytes=64 * 1024 * 1024),
             name="hartree",
-        )(rho.reshape(coarse, LANES), task_point, task_count, radial_index, fraction, angular, green)
+        )(rho.reshape(coarse, LANES), task_point, task_count, radial_index, fraction,
+          jnp.transpose(angular, (0, 2, 1, 3)), green)
         return out.reshape(share * LANES)
 
     in_specs = (

time: 25.7 us -> 23.7 us (0.922)
  local copies, waits for them, and re-layouts: 2.66 us -> 1.28 us
  Pallas kernels: 22.8 us -> 22.2 us
    unnamed x14 -> x1, local copies, waits for them, and re-layouts: 2.66 us -> 1.28 us
    pallas_call x1, Pallas kernels: 22.8 us -> 22.2 us  [per_device(): pl.pallas_call(functools.partial(kernel, n_shell, n_atom), out_shape=jax....]
where the time goes in v2:
time: 23.7 us; the launch traced here: 23.5 us
  Pallas kernels  22.2 us (94%)
  local copies, waits for them, and re-layouts  1.28 us (5%)
    pallas_call x1, Pallas kernels, per_device(): pl.pallas_call(functools.partial(kernel, n_shell, n_atom), out_shape=jax....  22.2 us
    unnamed x1, local copies, waits for them, and re-layouts  1.28 us

profile of v2, /device:TPU:0, one launch (start us, length us, event | category | flops | bytes accessed | tf_op | source)
XLA Modules:
  0.0 23.5 jit_solution(12785598685716626385)
XLA Ops:
  0.0 22.2 %hartree.1 = f32[8,128]{1,0:T(8,128)} custom-call(f32[32,128]{1,0:T(8,128)} %bitcast.5, s32[1,8,256]{2,1,0:T(8,128)} %pts_h.1, s32[1,8]{1,0:T(1,128)} %cnt_h.1, s32[1,8,256]{2,1,0:T(8,128)} %idx_h.1, f32[1,8,256]{2,1,0:T(8,128)} %frac_h.1, bf16[1,49,8,256]{3,2,1,0:T(8,128)(2,1)} %bitcast.3, f32[7,128,128]{2,1,0:T(8,128)} %green_h.1), custom_call_target="tpu_custom_call" | custom-call | tf_op jit(solution)/shard_map/hartree/pallas_call | solution.py:302
  22.2 1.3 %copy.9 = f32[1024]{0:T(1024)} copy(f32[1024]{0:T(1024)} %bitcast.4) | data formatting | bytes 8192

commit v3 on v2

v3 whole, which is shorter than its diff:
```python
import functools
import math

import jax
import jax.numpy as jnp
from jax import lax
from jax.experimental import pallas as pl
from jax.experimental.pallas import tpu as pltpu
from jax.sharding import PartitionSpec as P

MESH = pl.DeviceIdType.MESH
LANES = 128
NT = (((1,), (1,)), ((), ()))


def repeat(count, body):
    if count <= 16:
        for i in range(count):
            body(i)
    else:
        lax.fori_loop(0, count, lambda i, c: (body(i), c)[1], 0)


def accumulate(count, body, total):
    if count <= 16:
        for i in range(count):
            total = total + body(i)
        return total
    return lax.fori_loop(0, count, lambda i, c: c + body(i), total)


def split2(x):
    high = x.astype(jnp.bfloat16)
    low = (x - high.astype(jnp.float32)).astype(jnp.bfloat16)
    return high, low


def kernel(n_shell, n_atom, rho_h, pts_h, cnt_h, idx_h, frac_h, ang_h, green_h, out_ref,
           rho_v, pts_v, cnt_v, idx_v, frac_v, ang_s, ang_f, ang_v, green_v,
           live_v, low_v, high_v, onehot, meta_v, rmeta, rang, rows_v, gh_v, gl_v,
           mom_v, rmom, val_v, rval, part_v, rpart,
           local_sem, s_ang, r_ang, s_meta, r_meta, s_mom, r_mom, s_val, r_val, s_part, r_part):
    shell, ma = lax.axis_index("shell"), lax.axis_index("atom")
    half, own = val_v.shape[0], val_v.shape[1]
    me = lax.rem(shell, half)
    base = shell - me
    mirror = lax.rem(shell + half, n_shell)
    lm, atoms, slots = ang_s.shape
    lmp = rang.shape[2]
    body_rows = ang_v.shape[1]
    rest = lm - body_rows
    halves = slots // LANES
    degrees, width = green_v.shape[0], green_v.shape[1]
    coarse = rho_v.shape[0]

    def load(i, src, dst):
        copy = pltpu.make_async_copy(src, dst, local_sem.at[i])
        copy.start()
        return copy

    c_ang = load(0, ang_h.at[0], ang_s)
    c_pts = load(1, pts_h.at[0], pts_v)
    c_rho = load(2, rho_h, rho_v)
    c_idx = load(3, idx_h.at[0], idx_v)
    c_cnt = load(4, cnt_h, cnt_v)
    c_frac = load(5, frac_h.at[0], frac_v)
    c_green = load(6, green_h, green_v)

    def peer(k):
        return lax.rem(me + k, half)

    def atom_at(k):
        return lax.rem(ma + k, n_atom)

    def far_first(i):
        step = (i + 1) // 2
        return peer(half // 2 + step * (1 - 2 * (i % 2)))

    barrier = pltpu.get_barrier_semaphore()
    repeat(half - 1, lambda i: pl.semaphore_signal(
        barrier, inc=1, device_id=(base + peer(i + 1), ma), device_id_type=MESH))
    pl.semaphore_signal(barrier, inc=1, device_id=(mirror, ma), device_id_type=MESH)
    repeat(n_atom - 1, lambda i: pl.semaphore_signal(
        barrier, inc=1, device_id=(shell, atom_at(i + 1)), device_id_type=MESH))

    def ang_copy(t, to, slot):
        return pltpu.make_async_remote_copy(
            src_ref=ang_v.at[to * own + t], dst_ref=rang.at[t, slot, pl.ds(0, body_rows)],
            send_sem=s_ang.at[t, to], recv_sem=r_ang.at[t, slot],
            device_id=(base + to, ma), device_id_type=MESH)

    def meta_copy(to, slot):
        return pltpu.make_async_remote_copy(
            src_ref=meta_v.at[to], dst_ref=rmeta.at[slot],
            send_sem=s_meta.at[to], recv_sem=r_meta.at[slot],
            device_id=(base + to, ma), device_id_type=MESH)

    def mom_copy(t):
        return pltpu.make_async_remote_copy(
            src_ref=mom_v.at[t], dst_ref=rmom.at[t],
            send_sem=s_mom.at[t], recv_sem=r_mom.at[t],
            device_id=(mirror, ma), device_id_type=MESH)

    def val_copy(to, slot):
        return pltpu.make_async_remote_copy(
            src_ref=val_v.at[to], dst_ref=rval.at[slot],
            send_sem=s_val.at[to], recv_sem=r_val.at[slot],
            device_id=(base + to, ma), device_id_type=MESH)

    def part_copy(to, slot):
        return pltpu.make_async_remote_copy(
            src_ref=part_v.at[to], dst_ref=rpart.at[slot],
            send_sem=s_part.at[to], recv_sem=r_part.at[slot],
            device_id=(shell, to), device_id_type=MESH)

    c_ang.wait()

    def widen(m):
        at = pl.multiple_of(m * atoms, 8) if atoms % 8 == 0 else m * atoms
        for h in range(halves):
            ang_f[h, pl.ds(at, atoms), :] = ang_s[m, :, h * LANES:(h + 1) * LANES].astype(jnp.float32)

    def by_atom(a):
        for h in range(halves):
            ang_v[a, :, h * LANES:(h + 1) * LANES] = ang_f[
                h, pl.ds(a, body_rows, stride=atoms), :].astype(jnp.bfloat16)

    if atoms <= 16:
        for m in range(lm):
            widen(m)
    else:
        repeat(lm, widen)
    repeat(atoms, by_atom)
    pl.semaphore_wait(barrier, half + n_atom - 1)
    repeat(half - 1, lambda i: ang_copy(0, far_first(i), me).start())

    c_pts.wait()
    c_rho.wait()
    c_idx.wait()
    c_cnt.wait()
    c_frac.wait()
    low_v[...] = pts_v[...] & (LANES - 1)
    high_v[...] = pts_v[...] >> (LANES.bit_length() - 1)
    count_row = jnp.broadcast_to(cnt_v[...].astype(jnp.float32), (atoms, atoms))
    diagonal = (lax.broadcasted_iota(jnp.int32, (atoms, atoms), 0)
                == lax.broadcasted_iota(jnp.int32, (atoms, atoms), 1))
    counts = jnp.sum(jnp.where(diagonal, count_row, 0.0), axis=1, keepdims=True)
    slot_ids = lax.broadcasted_iota(jnp.int32, (atoms, slots), 1).astype(jnp.float32)
    live_v[...] = jnp.where(slot_ids < counts, idx_v[...].astype(jnp.float32), -8.0)

    rho = rho_v[...]
    rho_1 = rho.astype(jnp.bfloat16)
    rho_2, rho_3 = split2(rho - rho_1.astype(jnp.float32))
    rho_parts = jnp.concatenate(
        [rho_1.astype(jnp.float32), rho_2.astype(jnp.float32), rho_3.astype(jnp.float32)],
        axis=0).astype(jnp.bfloat16)
    fine_ids = lax.broadcasted_iota(jnp.int32, (LANES, slots), 0)
    coarse_ids = lax.broadcasted_iota(jnp.int32, (coarse, slots), 0)

    def build_meta(a):
        hot = jnp.where(fine_ids == low_v[pl.ds(a, 1), :], 1.0, 0.0).astype(jnp.bfloat16)
        onehot[a] = hot
        found = jnp.dot(rho_parts, hot, preferred_element_type=jnp.float32)
        found = found[0:coarse] + found[coarse:2 * coarse] + found[2 * coarse:3 * coarse]
        here = coarse_ids == high_v[pl.ds(a, 1), :]
        to, t = a // own, a % own
        meta_v[to, t, 0:1, :] = jnp.sum(jnp.where(here, found, 0.0), axis=0, keepdims=True)
        meta_v[to, t, 1:2, :] = live_v[pl.ds(a, 1), :]
        meta_v[to, t, 2:3, :] = frac_v[pl.ds(a, 1), :]
        for j in range(rest):
            for h in range(halves):
                meta_v[to, t, 3 + j:4 + j, h * LANES:(h + 1) * LANES] = ang_f[
                    h, pl.ds((body_rows + j) * atoms + a, 1), :]

    repeat(atoms, build_meta)
    repeat(half - 1, lambda i: meta_copy(far_first(i), me).start())
    for t in range(1, own):
        repeat(half - 1, lambda i: ang_copy(t, far_first(i), me).start())
    rmeta[me] = meta_v[me]
    for t in range(own):
        rang[t, me, 0:body_rows] = ang_v[me * own + t]

    c_green.wait()
    green = green_v[...].reshape(degrees * width, width)
    gh, gl = split2(green)
    gh_v[...] = gh
    gl_v[...] = gl

    grid_ids = lax.broadcasted_iota(jnp.int32, (width, slots), 0).astype(jnp.float32)
    tail_ids = lax.broadcasted_iota(jnp.int32, (lmp - body_rows, slots), 0)

    def add_batch(t, s):
        index, fraction = rmeta[s, t, 1:2, :], rmeta[s, t, 2:3, :]
        offset = grid_ids - index
        rows = jnp.where(offset == 0.0, 1.0 - fraction, jnp.where(offset == 1.0, fraction, 0.0))
        rows = rows.astype(jnp.bfloat16)
        rows_v[t, s] = rows
        tail = jnp.zeros((lmp - body_rows, slots), jnp.float32)
        for j in range(rest):
            tail = jnp.where(tail_ids == j, rmeta[s, t, 3 + j:4 + j, :], tail)
        rang[t, s, body_rows:lmp] = tail.astype(jnp.bfloat16)
        weighted = (rang[t, s].astype(jnp.float32) * rmeta[s, t, 0:1, :]).astype(jnp.bfloat16)
        return lax.dot_general(weighted, rows, NT, preferred_element_type=jnp.float32)

    def take_batch(t, i):
        s = peer(i + 1)
        if t == 0:
            meta_copy(me, s).wait_recv()
        ang_copy(t, me, s).wait_recv()
        return add_batch(t, s)

    partial = [add_batch(t, me) for t in range(own)]
    for t in range(own):
        partial[t] = accumulate(half - 1, functools.partial(take_batch, t), partial[t])
        mom_v[t] = partial[t].astype(jnp.bfloat16)
        mom_copy(t).start()

    row_ids = lax.broadcasted_iota(jnp.int32, (2 * lmp, width), 0)
    row_ids = jnp.where(row_ids >= lmp, row_ids - lmp, row_ids)

    def solve(mom):
        mom_h, mom_l = split2(mom)
        both = jnp.concatenate([mom_h.astype(jnp.float32), mom_l.astype(jnp.float32)], axis=0)
        spread = jnp.concatenate(
            [jnp.where((row_ids >= l * l) & (row_ids < (l + 1) * (l + 1)), both, 0.0)
             for l in range(degrees)], axis=1).astype(jnp.bfloat16)
        first = jnp.dot(spread, gh_v[...], preferred_element_type=jnp.float32)
        second = jnp.dot(spread[0:lmp], gl_v[...], preferred_element_type=jnp.float32)
        return (first[0:lmp] + first[lmp:] + second).astype(jnp.bfloat16)

    for t in range(own):
        mom_copy(t).wait_recv()
        table = solve(partial[t] + rmom[t].astype(jnp.float32))

        def evaluate(b, out):
            radial = jnp.dot(table, rows_v[t, b], preferred_element_type=jnp.float32)
            out[b, t] = jnp.sum(rang[t, b].astype(jnp.float32) * radial, axis=0, keepdims=True)

        repeat(half - 1, lambda i: evaluate(far_first(i), val_v))
        if t == own - 1:
            repeat(half - 1, lambda i: val_copy(far_first(i), me).start())
        evaluate(me, rval)

    def placed(a):
        spot = jnp.where(coarse_ids == high_v[pl.ds(a, 1), :], rval[a // own, a % own], 0.0)
        spot_h, spot_l = split2(spot)
        spots = jnp.concatenate(
            [spot_h.astype(jnp.float32), spot_l.astype(jnp.float32)], axis=0).astype(jnp.bfloat16)
        return lax.dot_general(spots, onehot[a], NT, preferred_element_type=jnp.float32)

    repeat(half - 1, lambda i: val_copy(me, peer(i + 1)).wait_recv())
    terms = accumulate(atoms - 1, lambda i: placed(i + 1), placed(0))
    terms = terms[0:coarse] + terms[coarse:]
    share = coarse // n_atom
    for g in range(n_atom):
        part_v[g] = terms[g * share:(g + 1) * share]

    repeat(n_atom - 1, lambda i: part_copy(atom_at(i + 1), ma).start())
    rpart[ma] = part_v[ma]
    repeat(n_atom - 1, lambda i: part_copy(ma, atom_at(i + 1)).wait_recv())
    total = rpart[0]
    for g in range(1, n_atom):
        total = total + rpart[g]
    out_ref[...] = total

    def finish(i):
        to = peer(i + 1)
        for t in range(own):
            ang_copy(t, to, me).wait_send()
        meta_copy(to, me).wait_send()
        val_copy(to, me).wait_send()

    repeat(half - 1, finish)
    for t in range(own):
        mom_copy(t).wait_send()
    repeat(n_atom - 1, lambda i: part_copy(atom_at(i + 1), ma).wait_send())


def solution(mesh):
    n_shell, n_atom = mesh.shape["shell"], mesh.shape["atom"]

    def per_device(rho, task_point, task_count, radial_index, fraction, angular, green):
        _, atoms, lm, slots = angular.shape
        points = rho.shape[0]
        degrees, width, _ = green.shape
        half = n_shell // 2
        own = atoms // half
        assert n_shell % 2 == 0 and atoms == half * own and points % (LANES * n_atom) == 0
        assert degrees == math.isqrt(lm)
        coarse = points // LANES
        share = coarse // n_atom
        lmp = (lm // 16 + 1) * 16
        meta_rows = 3 + lm % 16
        f32, bf16, i32 = jnp.float32, jnp.bfloat16, jnp.int32
        vmem = pltpu.VMEM
        scratch = [
            vmem((coarse, LANES), f32),
            vmem((atoms, slots), i32),
            vmem((1, atoms), i32),
            vmem((atoms, slots), i32),
            vmem((atoms, slots), f32),
            vmem((lm, atoms, slots), bf16),
            vmem((slots // LANES, lm * atoms, LANES), f32),
            vmem((atoms, lm // 16 * 16, slots), bf16),
            vmem((degrees, width, width), f32),
            vmem((atoms, slots), f32),
            vmem((atoms, slots), i32),
            vmem((atoms, slots), i32),
            vmem((atoms, LANES, slots), bf16),
            vmem((half, own, meta_rows, slots), f32),
            vmem((half, own, meta_rows, slots), f32),
            vmem((own, half, lmp, slots), bf16),
            vmem((own, half, width, slots), bf16),
            vmem((degrees * width, width), bf16),
            vmem((degrees * width, width), bf16),
            vmem((own, lmp, width), bf16),
            vmem((own, lmp, width), bf16),
            vmem((half, own, 1, slots), f32),
            vmem((half, own, 1, slots), f32),
            vmem((n_atom, share, LANES), f32),
            vmem((n_atom, share, LANES), f32),
        ] + [pltpu.SemaphoreType.DMA(shape) for shape in (
            (7,), (own, half), (own, half), (half,), (half,), (own,), (own,), (half,), (half,),
            (n_atom,), (n_atom,))]
        out = pl.pallas_call(
            functools.partial(kernel, n_shell, n_atom),
            out_shape=jax.ShapeDtypeStruct((share, LANES), f32),
            in_specs=[pl.BlockSpec(memory_space=pltpu.HBM)] * 7,
            out_specs=pl.BlockSpec(memory_space=pltpu.VMEM),
            scratch_shapes=scratch,
            compiler_params=pltpu.CompilerParams(
                collective_id=0, has_side_effects=True, vmem_limit_bytes=64 * 1024 * 1024),
            name="hartree",
        )(rho.reshape(coarse, LANES), task_point, task_count, radial_index, fraction,
          jnp.transpose(angular, (0, 2, 1, 3)), green)
        return out.reshape(share * LANES)

    in_specs = (
        P("shell"),
        P("shell", "atom", None),
        P("shell", "atom"),
        P("shell", "atom", None),
        P("shell", "atom", None),
        P("shell", "atom", None, None),
        P(),
    )
    return jax.shard_map(
        per_device, mesh=mesh, in_specs=in_specs, out_specs=P(("shell", "atom")), check_vma=False
    )
```

time: 23.7 us -> 22.5 us (0.949)
  Pallas kernels: 22.2 us -> 21 us
    pallas_call x1, Pallas kernels: 22.2 us -> 21 us  [per_device(): pl.pallas_call(functools.partial(kernel, n_shell, n_atom), out_shape=jax....]
where the time goes in v3:
time: 22.5 us; the launch traced here: 22.3 us
  Pallas kernels  21 us (93%)
  local copies, waits for them, and re-layouts  1.28 us (6%)
    pallas_call x1, Pallas kernels, per_device(): pl.pallas_call(functools.partial(kernel, n_shell, n_atom), out_shape=jax....  21 us
    unnamed x1, local copies, waits for them, and re-layouts  1.28 us

profile of v3, /device:TPU:0, one launch (start us, length us, event | category | flops | bytes accessed | tf_op | source)
XLA Modules:
  0.0 22.3 jit_solution(979363384671431318)
XLA Ops:
  0.0 21.0 %hartree.1 = f32[8,128]{1,0:T(8,128)} custom-call(f32[32,128]{1,0:T(8,128)} %bitcast.5, s32[1,8,256]{2,1,0:T(8,128)} %pts_h.1, s32[1,8]{1,0:T(1,128)} %cnt_h.1, s32[1,8,256]{2,1,0:T(8,128)} %idx_h.1, f32[1,8,256]{2,1,0:T(8,128)} %frac_h.1, bf16[1,49,8,256]{3,2,1,0:T(8,128)(2,1)} %bitcast.3, f32[7,128,128]{2,1,0:T(8,128)} %green_h.1), custom_call_target="tpu_custom_call" | custom-call | tf_op jit(solution)/shard_map/hartree/pallas_call | solution.py:325
  21.0 1.3 %copy.9 = f32[1024]{0:T(1024)} copy(f32[1024]{0:T(1024)} %bitcast.4) | data formatting | bytes 8192

commit v4 on v3

--- a/solution.py
+++ b/solution.py
@@ -10,6 +10,7 @@
 
 MESH = pl.DeviceIdType.MESH
 LANES = 128
+FINE = 32
 NT = (((1,), (1,)), ((), ()))
 
 
@@ -37,9 +38,9 @@
 
 def kernel(n_shell, n_atom, rho_h, pts_h, cnt_h, idx_h, frac_h, ang_h, green_h, out_ref,
            rho_v, pts_v, cnt_v, idx_v, frac_v, ang_s, ang_f, ang_v, green_v,
-           live_v, low_v, high_v, onehot, meta_v, rmeta, rang, rows_v, gh_v, gl_v,
-           mom_v, rmom, val_v, rval, part_v, rpart,
-           local_sem, s_ang, r_ang, s_meta, r_meta, s_mom, r_mom, s_val, r_val, s_part, r_part):
+           live_v, low_v, high_v, rpts, spot_v, onehot, meta_v, rmeta, rang, rows_v, gh_v, gl_v,
+           mom_v, rmom, val_v, rval,
+           local_sem, s_ang, r_ang, s_meta, r_meta, s_mom, r_mom, s_val, r_val, s_pts, r_pts):
     shell, ma = lax.axis_index("shell"), lax.axis_index("atom")
     half, own = val_v.shape[0], val_v.shape[1]
     me = lax.rem(shell, half)
@@ -80,8 +81,9 @@
     repeat(half - 1, lambda i: pl.semaphore_signal(
         barrier, inc=1, device_id=(base + peer(i + 1), ma), device_id_type=MESH))
     pl.semaphore_signal(barrier, inc=1, device_id=(mirror, ma), device_id_type=MESH)
-    repeat(n_atom - 1, lambda i: pl.semaphore_signal(
-        barrier, inc=1, device_id=(shell, atom_at(i + 1)), device_id_type=MESH))
+    for k in range(1, n_atom):
+        repeat(half, lambda i: pl.semaphore_signal(
+            barrier, inc=1, device_id=(base + peer(i), atom_at(k)), device_id_type=MESH))
 
     def ang_copy(t, to, slot):
         return pltpu.make_async_remote_copy(
@@ -101,17 +103,17 @@
             send_sem=s_mom.at[t], recv_sem=r_mom.at[t],
             device_id=(mirror, ma), device_id_type=MESH)
 
-    def val_copy(to, slot):
-        return pltpu.make_async_remote_copy(
-            src_ref=val_v.at[to], dst_ref=rval.at[slot],
-            send_sem=s_val.at[to], recv_sem=r_val.at[slot],
-            device_id=(base + to, ma), device_id_type=MESH)
-
-    def part_copy(to, slot):
-        return pltpu.make_async_remote_copy(
-            src_ref=part_v.at[to], dst_ref=rpart.at[slot],
-            send_sem=s_part.at[to], recv_sem=r_part.at[slot],
-            device_id=(shell, to), device_id_type=MESH)
+    def val_copy(to, group, slot, from_group):
+        return pltpu.make_async_remote_copy(
+            src_ref=val_v.at[to], dst_ref=rval.at[from_group, slot],
+            send_sem=s_val.at[group, to], recv_sem=r_val.at[from_group, slot],
+            device_id=(base + to, group), device_id_type=MESH)
+
+    def pts_copy(group, slot):
+        return pltpu.make_async_remote_copy(
+            src_ref=pts_v, dst_ref=rpts.at[slot],
+            send_sem=s_pts.at[group], recv_sem=r_pts.at[slot],
+            device_id=(shell, group), device_id_type=MESH)
 
     c_ang.wait()
 
@@ -131,10 +133,11 @@
     else:
         repeat(lm, widen)
     repeat(atoms, by_atom)
-    pl.semaphore_wait(barrier, half + n_atom - 1)
+    pl.semaphore_wait(barrier, half * n_atom)
     repeat(half - 1, lambda i: ang_copy(0, far_first(i), me).start())
 
     c_pts.wait()
+    repeat(n_atom - 1, lambda i: pts_copy(atom_at(i + 1), ma).start())
     c_rho.wait()
     c_idx.wait()
     c_cnt.wait()
@@ -159,7 +162,6 @@
 
     def build_meta(a):
         hot = jnp.where(fine_ids == low_v[pl.ds(a, 1), :], 1.0, 0.0).astype(jnp.bfloat16)
-        onehot[a] = hot
         found = jnp.dot(rho_parts, hot, preferred_element_type=jnp.float32)
         found = found[0:coarse] + found[coarse:2 * coarse] + found[2 * coarse:3 * coarse]
         here = coarse_ids == high_v[pl.ds(a, 1), :]
@@ -177,6 +179,7 @@
     for t in range(1, own):
         repeat(half - 1, lambda i: ang_copy(t, far_first(i), me).start())
     rmeta[me] = meta_v[me]
+    rpts[ma] = pts_v[...]
     for t in range(own):
         rang[t, me, 0:body_rows] = ang_v[me * own + t]
 
@@ -215,65 +218,104 @@
         mom_v[t] = partial[t].astype(jnp.bfloat16)
         mom_copy(t).start()
 
-    row_ids = lax.broadcasted_iota(jnp.int32, (2 * lmp, width), 0)
-    row_ids = jnp.where(row_ids >= lmp, row_ids - lmp, row_ids)
-
-    def solve(mom):
-        mom_h, mom_l = split2(mom)
-        both = jnp.concatenate([mom_h.astype(jnp.float32), mom_l.astype(jnp.float32)], axis=0)
-        spread = jnp.concatenate(
-            [jnp.where((row_ids >= l * l) & (row_ids < (l + 1) * (l + 1)), both, 0.0)
+    share = out_ref.shape[0]
+    cells = LANES // FINE
+    cell_ids = lax.broadcasted_iota(jnp.int32, (FINE, slots), 0)
+
+    def find_spots(k):
+        group = atom_at(k)
+        if k > 0:
+            pts_copy(ma, group).wait_recv()
+        at = rpts[group] - ma * (share * LANES)
+        block = at >> (LANES.bit_length() - 1)
+        inside = (block >= 0) & (block < share)
+        cell = (at >> (FINE.bit_length() - 1)) & (cells - 1)
+        spot_v[group] = jnp.where(inside, cell * share + block, -1)
+        rpts[group] = at & (FINE - 1)
+
+        def mark(a):
+            column = rpts[group, pl.ds(a, 1), :]
+            onehot[group, a] = jnp.where(cell_ids == column, 1.0, 0.0).astype(jnp.bfloat16)
+
+        repeat(atoms, mark)
+
+    for k in range(n_atom):
+        find_spots(k)
+
+    def spread_of(mom):
+        rows = mom.shape[0]
+        ids = lax.broadcasted_iota(jnp.int32, (rows, width), 0)
+        ids = jnp.where(ids >= lmp, ids - lmp, ids)
+        return jnp.concatenate(
+            [jnp.where((ids >= l * l) & (ids < (l + 1) * (l + 1)), mom, 0.0)
              for l in range(degrees)], axis=1).astype(jnp.bfloat16)
+
+    solved = []
+    for t in range(own):
+        mom_h, mom_l = split2(partial[t])
+        spread = spread_of(
+            jnp.concatenate([mom_h.astype(jnp.float32), mom_l.astype(jnp.float32)], axis=0))
         first = jnp.dot(spread, gh_v[...], preferred_element_type=jnp.float32)
         second = jnp.dot(spread[0:lmp], gl_v[...], preferred_element_type=jnp.float32)
-        return (first[0:lmp] + first[lmp:] + second).astype(jnp.bfloat16)
+        solved.append(first[0:lmp] + first[lmp:] + second)
 
     for t in range(own):
         mom_copy(t).wait_recv()
-        table = solve(partial[t] + rmom[t].astype(jnp.float32))
-
-        def evaluate(b, out):
+        spread = spread_of(rmom[t].astype(jnp.float32))
+        other = (jnp.dot(spread, gh_v[...], preferred_element_type=jnp.float32)
+                 + jnp.dot(spread, gl_v[...], preferred_element_type=jnp.float32))
+        table = (solved[t] + other).astype(jnp.bfloat16)
+
+        def evaluate(b):
             radial = jnp.dot(table, rows_v[t, b], preferred_element_type=jnp.float32)
-            out[b, t] = jnp.sum(rang[t, b].astype(jnp.float32) * radial, axis=0, keepdims=True)
-
-        repeat(half - 1, lambda i: evaluate(far_first(i), val_v))
-        if t == own - 1:
-            repeat(half - 1, lambda i: val_copy(far_first(i), me).start())
-        evaluate(me, rval)
-
-    def placed(a):
-        spot = jnp.where(coarse_ids == high_v[pl.ds(a, 1), :], rval[a // own, a % own], 0.0)
-        spot_h, spot_l = split2(spot)
-        spots = jnp.concatenate(
-            [spot_h.astype(jnp.float32), spot_l.astype(jnp.float32)], axis=0).astype(jnp.bfloat16)
-        return lax.dot_general(spots, onehot[a], NT, preferred_element_type=jnp.float32)
-
-    repeat(half - 1, lambda i: val_copy(me, peer(i + 1)).wait_recv())
-    terms = accumulate(atoms - 1, lambda i: placed(i + 1), placed(0))
-    terms = terms[0:coarse] + terms[coarse:]
-    share = coarse // n_atom
-    for g in range(n_atom):
-        part_v[g] = terms[g * share:(g + 1) * share]
-
-    repeat(n_atom - 1, lambda i: part_copy(atom_at(i + 1), ma).start())
-    rpart[ma] = part_v[ma]
-    repeat(n_atom - 1, lambda i: part_copy(ma, atom_at(i + 1)).wait_recv())
-    total = rpart[0]
-    for g in range(1, n_atom):
-        total = total + rpart[g]
-    out_ref[...] = total
+            val_v[b, t] = jnp.sum(rang[t, b].astype(jnp.float32) * radial, axis=0, keepdims=True)
+
+        repeat(half - 1, lambda i: evaluate(far_first(i)))
+        evaluate(me)
+    repeat(half - 1, lambda i: val_copy(far_first(i), ma, me, ma).start())
+    for k in range(1, n_atom):
+        repeat(half, lambda i: val_copy(peer(half - 1 - i), atom_at(k), me, ma).start())
+    rval[ma, me] = val_v[me]
+
+    spot_ids = lax.broadcasted_iota(jnp.int32, (cells * share, slots), 0)
+
+    def add_group(k, terms):
+        group = atom_at(k)
+        if k == 0:
+            repeat(half - 1, lambda i: val_copy(me, ma, peer(i + 1), ma).wait_recv())
+        else:
+            repeat(half, lambda i: val_copy(me, ma, peer(i), group).wait_recv())
+
+        def placed(a):
+            here = spot_ids == spot_v[group, pl.ds(a, 1), :]
+            spot = jnp.where(here, rval[group, a // own, a % own], 0.0)
+            spot_h, spot_l = split2(spot)
+            spots = jnp.concatenate(
+                [spot_h.astype(jnp.float32), spot_l.astype(jnp.float32)], axis=0).astype(jnp.bfloat16)
+            return lax.dot_general(spots, onehot[group, a], NT, preferred_element_type=jnp.float32)
+
+        return accumulate(atoms, placed, terms)
+
+    terms = jnp.zeros((2 * cells * share, FINE), jnp.float32)
+    for k in range(n_atom):
+        terms = add_group(k, terms)
+    terms = terms[0:cells * share] + terms[cells * share:]
+    out_ref[...] = jnp.concatenate(
+        [terms[c * share:(c + 1) * share] for c in range(cells)], axis=1)
 
     def finish(i):
         to = peer(i + 1)
         for t in range(own):
             ang_copy(t, to, me).wait_send()
         meta_copy(to, me).wait_send()
-        val_copy(to, me).wait_send()
+        val_copy(to, ma, me, ma).wait_send()
 
     repeat(half - 1, finish)
     for t in range(own):
         mom_copy(t).wait_send()
-    repeat(n_atom - 1, lambda i: part_copy(atom_at(i + 1), ma).wait_send())
+    for k in range(1, n_atom):
+        pts_copy(atom_at(k), ma).wait_send()
+        repeat(half, lambda i: val_copy(peer(i), atom_at(k), me, ma).wait_send())
 
 
 def solution(mesh):
@@ -306,7 +348,9 @@
             vmem((atoms, slots), f32),
             vmem((atoms, slots), i32),
             vmem((atoms, slots), i32),
-            vmem((atoms, LANES, slots), bf16),
+            vmem((n_atom, atoms, slots), i32),
+            vmem((n_atom, atoms, slots), i32),
+            vmem((n_atom, atoms, FINE, slots), bf16),
             vmem((half, own, meta_rows, slots), f32),
             vmem((half, own, meta_rows, slots), f32),
             vmem((own, half, lmp, slots), bf16),
@@ -316,23 +360,22 @@
             vmem((own, lmp, width), bf16),
             vmem((own, lmp, width), bf16),
             vmem((half, own, 1, slots), f32),
-            vmem((half, own, 1, slots), f32),
-            vmem((n_atom, share, LANES), f32),
-            vmem((n_atom, share, LANES), f32),
+            vmem((n_atom, half, own, 1, slots), f32),
         ] + [pltpu.SemaphoreType.DMA(shape) for shape in (
-            (7,), (own, half), (own, half), (half,), (half,), (own,), (own,), (half,), (half,),
-            (n_atom,), (n_atom,))]
+            (7,), (own, half), (own, half), (half,), (half,), (own,), (own,), (n_atom, half),
+            (n_atom, half), (n_atom,), (n_atom,))]
         out = pl.pallas_call(
             functools.partial(kernel, n_shell, n_atom),
-            out_shape=jax.ShapeDtypeStruct((share, LANES), f32),
+            out_shape=pltpu.VMEM((share, LANES), f32),
             in_specs=[pl.BlockSpec(memory_space=pltpu.HBM)] * 7,
             out_specs=pl.BlockSpec(memory_space=pltpu.VMEM),
             scratch_shapes=scratch,
             compiler_params=pltpu.CompilerParams(
-                collective_id=0, has_side_effects=True, vmem_limit_bytes=64 * 1024 * 1024),
+                collective_id=0, has_side_effects=True, vmem_limit_bytes=48 * 1024 * 1024),
             name="hartree",
-        )(rho.reshape(coarse, LANES), task_point, task_count, radial_index, fraction,
-          jnp.transpose(angular, (0, 2, 1, 3)), green)
+        )(*[pltpu.with_memory_space_constraint(x, pltpu.HBM) for x in (
+            rho.reshape(coarse, LANES), task_point, task_count, radial_index, fraction,
+            jnp.transpose(angular, (0, 2, 1, 3)), green)])
         return out.reshape(share * LANES)
 
     in_specs = (

time: 22.5 us -> 20.2 us (0.90)
  Pallas kernels: 21 us -> 19.4 us
  local copies, waits for them, and re-layouts: 1.28 us -> 0.6 us
    pallas_call x1, Pallas kernels: 21 us -> 19.4 us  [per_device(): pl.pallas_call(functools.partial(kernel, n_shell, n_atom), out_shape=pltp...]
    unnamed x1, local copies, waits for them, and re-layouts: 1.28 us -> 0.6 us
where the time goes in v4:
time: 20.2 us; the launch traced here: 20.1 us
  Pallas kernels  19.4 us (96%)
  local copies, waits for them, and re-layouts  0.6 us (3%)
    pallas_call x1, Pallas kernels, per_device(): pl.pallas_call(functools.partial(kernel, n_shell, n_atom), out_shape=pltp...  19.4 us
    unnamed x1, local copies, waits for them, and re-layouts  0.6 us

profile of v4, /device:TPU:0, one launch (start us, length us, event | category | flops | bytes accessed | tf_op | source)
XLA Modules:
  0.0 20.1 jit_solution(8042224396168236413)
XLA Ops:
  0.0 19.4 %hartree.1 = f32[8,128]{1,0:T(8,128)S(1)} custom-call(f32[32,128]{1,0:T(8,128)} %bitcast.5, s32[1,8,256]{2,1,0:T(8,128)} %pts_h.1, s32[1,8]{1,0:T(1,128)} %cnt_h.1, s32[1,8,256]{2,1,0:T(8,128)} %idx_h.1, f32[1,8,256]{2,1,0:T(8,128)} %frac_h.1, bf16[1,49,8,256]{3,2,1,0:T(8,128)(2,1)} %bitcast.4, f32[7,128,128]{2,1,0:T(8,128)} %green_h.1), custom_call_target="tpu_custom_call" | custom-call | tf_op jit(solution)/shard_map/hartree/pallas_call | solution.py:367
  19.5 0.6 %copy.9 = f32[1024]{0:T(1024)} copy(f32[1024]{0:T(1024)S(1)} %bitcast.3) | data formatting | bytes 8192

commit v5 on v4

--- a/solution.py
+++ b/solution.py
@@ -11,6 +11,7 @@
 MESH = pl.DeviceIdType.MESH
 LANES = 128
 FINE = 32
+PIECES = 4
 NT = (((1,), (1,)), ((), ()))
 
 
@@ -38,7 +39,7 @@
 
 def kernel(n_shell, n_atom, rho_h, pts_h, cnt_h, idx_h, frac_h, ang_h, green_h, out_ref,
            rho_v, pts_v, cnt_v, idx_v, frac_v, ang_s, ang_f, ang_v, green_v,
-           live_v, low_v, high_v, rpts, spot_v, onehot, meta_v, rmeta, rang, rows_v, gh_v, gl_v,
+           live_v, low_v, high_v, rpts, spot_v, onehot, meta_v, rmeta, rang, rows_v, green_2,
            mom_v, rmom, val_v, rval,
            local_sem, s_ang, r_ang, s_meta, r_meta, s_mom, r_mom, s_val, r_val, s_pts, r_pts):
     shell, ma = lax.axis_index("shell"), lax.axis_index("atom")
@@ -59,13 +60,14 @@
         copy.start()
         return copy
 
-    c_ang = load(0, ang_h.at[0], ang_s)
-    c_pts = load(1, pts_h.at[0], pts_v)
-    c_rho = load(2, rho_h, rho_v)
-    c_idx = load(3, idx_h.at[0], idx_v)
-    c_cnt = load(4, cnt_h, cnt_v)
-    c_frac = load(5, frac_h.at[0], frac_v)
-    c_green = load(6, green_h, green_v)
+    bounds = [lm * i // PIECES for i in range(PIECES + 1)]
+    c_ang = [load(6 + i, ang_h.at[0, pl.ds(low, high - low)], ang_s.at[pl.ds(low, high - low)])
+             for i, (low, high) in enumerate(zip(bounds, bounds[1:]))]
+    c_pts = load(0, pts_h.at[0], pts_v)
+    c_rho = load(1, rho_h, rho_v)
+    c_idx = load(2, idx_h.at[0], idx_v)
+    c_cnt = load(3, cnt_h, cnt_v)
+    c_frac = load(4, frac_h.at[0], frac_v)
 
     def peer(k):
         return lax.rem(me + k, half)
@@ -84,6 +86,7 @@
     for k in range(1, n_atom):
         repeat(half, lambda i: pl.semaphore_signal(
             barrier, inc=1, device_id=(base + peer(i), atom_at(k)), device_id_type=MESH))
+    c_green = load(5, green_h, green_v)
 
     def ang_copy(t, to, slot):
         return pltpu.make_async_remote_copy(
@@ -114,8 +117,6 @@
             src_ref=pts_v, dst_ref=rpts.at[slot],
             send_sem=s_pts.at[group], recv_sem=r_pts.at[slot],
             device_id=(shell, group), device_id_type=MESH)
-
-    c_ang.wait()
 
     def widen(m):
         at = pl.multiple_of(m * atoms, 8) if atoms % 8 == 0 else m * atoms
@@ -127,11 +128,9 @@
             ang_v[a, :, h * LANES:(h + 1) * LANES] = ang_f[
                 h, pl.ds(a, body_rows, stride=atoms), :].astype(jnp.bfloat16)
 
-    if atoms <= 16:
-        for m in range(lm):
-            widen(m)
-    else:
-        repeat(lm, widen)
+    for copy, low, high in zip(c_ang, bounds, bounds[1:]):
+        copy.wait()
+        repeat(high - low, lambda i: widen(low + i))
     repeat(atoms, by_atom)
     pl.semaphore_wait(barrier, half * n_atom)
     repeat(half - 1, lambda i: ang_copy(0, far_first(i), me).start())
@@ -186,37 +185,60 @@
     c_green.wait()
     green = green_v[...].reshape(degrees * width, width)
     gh, gl = split2(green)
-    gh_v[...] = gh
-    gl_v[...] = gl
+    green_2[:, 0:width] = gh
+    green_2[:, width:2 * width] = gl
 
     grid_ids = lax.broadcasted_iota(jnp.int32, (width, slots), 0).astype(jnp.float32)
     tail_ids = lax.broadcasted_iota(jnp.int32, (lmp - body_rows, slots), 0)
 
-    def add_batch(t, s):
+    def make_rows(t, s):
         index, fraction = rmeta[s, t, 1:2, :], rmeta[s, t, 2:3, :]
         offset = grid_ids - index
         rows = jnp.where(offset == 0.0, 1.0 - fraction, jnp.where(offset == 1.0, fraction, 0.0))
-        rows = rows.astype(jnp.bfloat16)
-        rows_v[t, s] = rows
+        rows_v[t, s] = rows.astype(jnp.bfloat16)
         tail = jnp.zeros((lmp - body_rows, slots), jnp.float32)
         for j in range(rest):
             tail = jnp.where(tail_ids == j, rmeta[s, t, 3 + j:4 + j, :], tail)
         rang[t, s, body_rows:lmp] = tail.astype(jnp.bfloat16)
+
+    def add_batch(t, s):
         weighted = (rang[t, s].astype(jnp.float32) * rmeta[s, t, 0:1, :]).astype(jnp.bfloat16)
-        return lax.dot_general(weighted, rows, NT, preferred_element_type=jnp.float32)
+        return lax.dot_general(weighted, rows_v[t, s], NT, preferred_element_type=jnp.float32)
 
     def take_batch(t, i):
         s = peer(i + 1)
         if t == 0:
             meta_copy(me, s).wait_recv()
+            make_rows(t, s)
         ang_copy(t, me, s).wait_recv()
         return add_batch(t, s)
 
+    def solve(mom):
+        rows = mom.shape[0]
+        ids = lax.broadcasted_iota(jnp.int32, (rows, width), 0)
+        ids = jnp.where(ids >= lmp, ids - lmp, ids)
+        spread = jnp.concatenate(
+            [jnp.where((ids >= l * l) & (ids < (l + 1) * (l + 1)), mom, 0.0)
+             for l in range(degrees)], axis=1).astype(jnp.bfloat16)
+        both = jnp.dot(spread, green_2[...], preferred_element_type=jnp.float32)
+        return both[:, 0:width] + both[:, width:]
+
+    def solve_own(mom):
+        mom_h, mom_l = split2(mom)
+        both = solve(jnp.concatenate([mom_h.astype(jnp.float32), mom_l.astype(jnp.float32)], axis=0))
+        return both[0:lmp] + both[lmp:]
+
+    for t in range(own):
+        make_rows(t, me)
     partial = [add_batch(t, me) for t in range(own)]
+    solved = []
     for t in range(own):
         partial[t] = accumulate(half - 1, functools.partial(take_batch, t), partial[t])
         mom_v[t] = partial[t].astype(jnp.bfloat16)
         mom_copy(t).start()
+        if t + 1 < own:
+            repeat(half - 1, lambda i: make_rows(t + 1, peer(i + 1)))
+        solved.append(solve_own(partial[t]))
 
     share = out_ref.shape[0]
     cells = LANES // FINE
@@ -242,29 +264,9 @@
     for k in range(n_atom):
         find_spots(k)
 
-    def spread_of(mom):
-        rows = mom.shape[0]
-        ids = lax.broadcasted_iota(jnp.int32, (rows, width), 0)
-        ids = jnp.where(ids >= lmp, ids - lmp, ids)
-        return jnp.concatenate(
-            [jnp.where((ids >= l * l) & (ids < (l + 1) * (l + 1)), mom, 0.0)
-             for l in range(degrees)], axis=1).astype(jnp.bfloat16)
-
-    solved = []
-    for t in range(own):
-        mom_h, mom_l = split2(partial[t])
-        spread = spread_of(
-            jnp.concatenate([mom_h.astype(jnp.float32), mom_l.astype(jnp.float32)], axis=0))
-        first = jnp.dot(spread, gh_v[...], preferred_element_type=jnp.float32)
-        second = jnp.dot(spread[0:lmp], gl_v[...], preferred_element_type=jnp.float32)
-        solved.append(first[0:lmp] + first[lmp:] + second)
-
     for t in range(own):
         mom_copy(t).wait_recv()
-        spread = spread_of(rmom[t].astype(jnp.float32))
-        other = (jnp.dot(spread, gh_v[...], preferred_element_type=jnp.float32)
-                 + jnp.dot(spread, gl_v[...], preferred_element_type=jnp.float32))
-        table = (solved[t] + other).astype(jnp.bfloat16)
+        table = (solved[t] + solve(rmom[t].astype(jnp.float32))).astype(jnp.bfloat16)
 
         def evaluate(b):
             radial = jnp.dot(table, rows_v[t, b], preferred_element_type=jnp.float32)
@@ -288,10 +290,10 @@
 
         def placed(a):
             here = spot_ids == spot_v[group, pl.ds(a, 1), :]
-            spot = jnp.where(here, rval[group, a // own, a % own], 0.0)
-            spot_h, spot_l = split2(spot)
+            value_h, value_l = split2(rval[group, a // own, a % own])
             spots = jnp.concatenate(
-                [spot_h.astype(jnp.float32), spot_l.astype(jnp.float32)], axis=0).astype(jnp.bfloat16)
+                [jnp.where(here, value_h.astype(jnp.float32), 0.0),
+                 jnp.where(here, value_l.astype(jnp.float32), 0.0)], axis=0).astype(jnp.bfloat16)
             return lax.dot_general(spots, onehot[group, a], NT, preferred_element_type=jnp.float32)
 
         return accumulate(atoms, placed, terms)
@@ -355,14 +357,13 @@
             vmem((half, own, meta_rows, slots), f32),
             vmem((own, half, lmp, slots), bf16),
             vmem((own, half, width, slots), bf16),
-            vmem((degrees * width, width), bf16),
-            vmem((degrees * width, width), bf16),
+            vmem((degrees * width, 2 * width), bf16),
             vmem((own, lmp, width), bf16),
             vmem((own, lmp, width), bf16),
             vmem((half, own, 1, slots), f32),
             vmem((n_atom, half, own, 1, slots), f32),
         ] + [pltpu.SemaphoreType.DMA(shape) for shape in (
-            (7,), (own, half), (own, half), (half,), (half,), (own,), (own,), (n_atom, half),
+            (6 + PIECES,), (own, half), (own, half), (half,), (half,), (own,), (own,), (n_atom, half),
             (n_atom, half), (n_atom,), (n_atom,))]
         out = pl.pallas_call(
             functools.partial(kernel, n_shell, n_atom),

time: 20.2 us -> 20.6 us (1.020)
  Pallas kernels: 19.4 us -> 19.8 us
    pallas_call x1, Pallas kernels: 19.4 us -> 19.8 us  [per_device(): pl.pallas_call(functools.partial(kernel, n_shell, n_atom), out_shape=pltp...]
where the time goes in v5:
time: 20.6 us; the launch traced here: 20.4 us
  Pallas kernels  19.8 us (96%)
  local copies, waits for them, and re-layouts  0.6 us (3%)
    pallas_call x1, Pallas kernels, per_device(): pl.pallas_call(functools.partial(kernel, n_shell, n_atom), out_shape=pltp...  19.8 us
    unnamed x1, local copies, waits for them, and re-layouts  0.6 us

profile of v5, /device:TPU:0, one launch (start us, length us, event | category | flops | bytes accessed | tf_op | source)
XLA Modules:
  0.0 20.4 jit_solution(18311817588413319801)
XLA Ops:
  0.0 19.8 %hartree.1 = f32[8,128]{1,0:T(8,128)S(1)} custom-call(f32[32,128]{1,0:T(8,128)} %bitcast.5, s32[1,8,256]{2,1,0:T(8,128)} %pts_h.1, s32[1,8]{1,0:T(1,128)} %cnt_h.1, s32[1,8,256]{2,1,0:T(8,128)} %idx_h.1, f32[1,8,256]{2,1,0:T(8,128)} %frac_h.1, bf16[1,49,8,256]{3,2,1,0:T(8,128)(2,1)} %bitcast.4, f32[7,128,128]{2,1,0:T(8,128)} %green_h.1), custom_call_target="tpu_custom_call" | custom-call | tf_op jit(solution)/shard_map/hartree/pallas_call | solution.py:368
  19.8 0.6 %copy.9 = f32[1024]{0:T(1024)} copy(f32[1024]{0:T(1024)S(1)} %bitcast.3) | data formatting | bytes 8192

commit v6 on v5

--- a/solution.py
+++ b/solution.py
@@ -10,8 +10,8 @@
 
 MESH = pl.DeviceIdType.MESH
 LANES = 128
-FINE = 32
-PIECES = 4
+FINE = 64
+PIECES = 1
 NT = (((1,), (1,)), ((), ()))
 
 
@@ -83,9 +83,8 @@
     repeat(half - 1, lambda i: pl.semaphore_signal(
         barrier, inc=1, device_id=(base + peer(i + 1), ma), device_id_type=MESH))
     pl.semaphore_signal(barrier, inc=1, device_id=(mirror, ma), device_id_type=MESH)
-    for k in range(1, n_atom):
-        repeat(half, lambda i: pl.semaphore_signal(
-            barrier, inc=1, device_id=(base + peer(i), atom_at(k)), device_id_type=MESH))
+    repeat(n_atom - 1, lambda i: pl.semaphore_signal(
+        barrier, inc=1, device_id=(shell, atom_at(i + 1)), device_id_type=MESH))
     c_green = load(5, green_h, green_v)
 
     def ang_copy(t, to, slot):
@@ -109,7 +108,7 @@
     def val_copy(to, group, slot, from_group):
         return pltpu.make_async_remote_copy(
             src_ref=val_v.at[to], dst_ref=rval.at[from_group, slot],
-            send_sem=s_val.at[group, to], recv_sem=r_val.at[from_group, slot],
+            send_sem=s_val.at[group], recv_sem=r_val.at[from_group],
             device_id=(base + to, group), device_id_type=MESH)
 
     def pts_copy(group, slot):
@@ -132,7 +131,7 @@
         copy.wait()
         repeat(high - low, lambda i: widen(low + i))
     repeat(atoms, by_atom)
-    pl.semaphore_wait(barrier, half * n_atom)
+    pl.semaphore_wait(barrier, half + n_atom - 1)
     repeat(half - 1, lambda i: ang_copy(0, far_first(i), me).start())
 
     c_pts.wait()
@@ -231,14 +230,12 @@
     for t in range(own):
         make_rows(t, me)
     partial = [add_batch(t, me) for t in range(own)]
-    solved = []
     for t in range(own):
         partial[t] = accumulate(half - 1, functools.partial(take_batch, t), partial[t])
         mom_v[t] = partial[t].astype(jnp.bfloat16)
         mom_copy(t).start()
         if t + 1 < own:
             repeat(half - 1, lambda i: make_rows(t + 1, peer(i + 1)))
-        solved.append(solve_own(partial[t]))
 
     share = out_ref.shape[0]
     cells = LANES // FINE
@@ -264,6 +261,17 @@
     for k in range(n_atom):
         find_spots(k)
 
+    solved = [solve_own(partial[t]) for t in range(own)]
+
+    def sent(i):
+        to = peer(i + 1)
+        for t in range(own):
+            ang_copy(t, to, me).wait_send()
+        meta_copy(to, me).wait_send()
+
+    repeat(half - 1, sent)
+    repeat(n_atom - 1, lambda i: pts_copy(atom_at(i + 1), ma).wait_send())
+
     for t in range(own):
         mom_copy(t).wait_recv()
         table = (solved[t] + solve(rmom[t].astype(jnp.float32))).astype(jnp.bfloat16)
@@ -279,14 +287,20 @@
         repeat(half, lambda i: val_copy(peer(half - 1 - i), atom_at(k), me, ma).start())
     rval[ma, me] = val_v[me]
 
+    def val_batch(group, first, count):
+        return pltpu.make_async_remote_copy(
+            src_ref=val_v.at[pl.ds(first, count)], dst_ref=rval.at[group, pl.ds(first, count)],
+            send_sem=s_val.at[group], recv_sem=r_val.at[group],
+            device_id=(mirror, ma), device_id_type=MESH)
+
     spot_ids = lax.broadcasted_iota(jnp.int32, (cells * share, slots), 0)
 
     def add_group(k, terms):
         group = atom_at(k)
         if k == 0:
-            repeat(half - 1, lambda i: val_copy(me, ma, peer(i + 1), ma).wait_recv())
+            val_batch(ma, 0, half - 1).wait_recv()
         else:
-            repeat(half, lambda i: val_copy(me, ma, peer(i), group).wait_recv())
+            val_batch(group, 0, half).wait_recv()
 
         def placed(a):
             here = spot_ids == spot_v[group, pl.ds(a, 1), :]
@@ -305,19 +319,11 @@
     out_ref[...] = jnp.concatenate(
         [terms[c * share:(c + 1) * share] for c in range(cells)], axis=1)
 
-    def finish(i):
-        to = peer(i + 1)
-        for t in range(own):
-            ang_copy(t, to, me).wait_send()
-        meta_copy(to, me).wait_send()
-        val_copy(to, ma, me, ma).wait_send()
-
-    repeat(half - 1, finish)
+    val_batch(ma, 0, half - 1).wait_send()
+    for k in range(1, n_atom):
+        val_batch(atom_at(k), 0, half).wait_send()
     for t in range(own):
         mom_copy(t).wait_send()
-    for k in range(1, n_atom):
-        pts_copy(atom_at(k), ma).wait_send()
-        repeat(half, lambda i: val_copy(peer(i), atom_at(k), me, ma).wait_send())
 
 
 def solution(mesh):
@@ -363,8 +369,8 @@
             vmem((half, own, 1, slots), f32),
             vmem((n_atom, half, own, 1, slots), f32),
         ] + [pltpu.SemaphoreType.DMA(shape) for shape in (
-            (6 + PIECES,), (own, half), (own, half), (half,), (half,), (own,), (own,), (n_atom, half),
-            (n_atom, half), (n_atom,), (n_atom,))]
+            (6 + PIECES,), (own, half), (own, half), (half,), (half,), (own,), (own,), (n_atom,),
+            (n_atom,), (n_atom,), (n_atom,))]
         out = pl.pallas_call(
             functools.partial(kernel, n_shell, n_atom),
             out_shape=pltpu.VMEM((share, LANES), f32),

time: 20.6 us -> 19.2 us (0.932)
  Pallas kernels: 19.8 us -> 18.4 us
    pallas_call x1, Pallas kernels: 19.8 us -> 18.4 us  [per_device(): pl.pallas_call(functools.partial(kernel, n_shell, n_atom), out_shape=pltp...]
where the time goes in v6:
time: 19.2 us; the launch traced here: 19 us
  Pallas kernels  18.4 us (96%)
  local copies, waits for them, and re-layouts  0.6 us (3%)
    pallas_call x1, Pallas kernels, per_device(): pl.pallas_call(functools.partial(kernel, n_shell, n_atom), out_shape=pltp...  18.4 us
    unnamed x1, local copies, waits for them, and re-layouts  0.6 us

profile of v6, /device:TPU:0, one launch (start us, length us, event | category | flops | bytes accessed | tf_op | source)
XLA Modules:
  0.0 19.0 jit_solution(12721401007813219688)
XLA Ops:
  0.0 18.4 %hartree.1 = f32[8,128]{1,0:T(8,128)S(1)} custom-call(f32[32,128]{1,0:T(8,128)} %bitcast.5, s32[1,8,256]{2,1,0:T(8,128)} %pts_h.1, s32[1,8]{1,0:T(1,128)} %cnt_h.1, s32[1,8,256]{2,1,0:T(8,128)} %idx_h.1, f32[1,8,256]{2,1,0:T(8,128)} %frac_h.1, bf16[1,49,8,256]{3,2,1,0:T(8,128)(2,1)} %bitcast.4, f32[7,128,128]{2,1,0:T(8,128)} %green_h.1), custom_call_target="tpu_custom_call" | custom-call | tf_op jit(solution)/shard_map/hartree/pallas_call | solution.py:374
  18.4 0.6 %copy.9 = f32[1024]{0:T(1024)} copy(f32[1024]{0:T(1024)S(1)} %bitcast.3) | data formatting | bytes 8192

commit v7 on v6

--- a/solution.py
+++ b/solution.py
@@ -63,11 +63,6 @@
     bounds = [lm * i // PIECES for i in range(PIECES + 1)]
     c_ang = [load(6 + i, ang_h.at[0, pl.ds(low, high - low)], ang_s.at[pl.ds(low, high - low)])
              for i, (low, high) in enumerate(zip(bounds, bounds[1:]))]
-    c_pts = load(0, pts_h.at[0], pts_v)
-    c_rho = load(1, rho_h, rho_v)
-    c_idx = load(2, idx_h.at[0], idx_v)
-    c_cnt = load(3, cnt_h, cnt_v)
-    c_frac = load(4, frac_h.at[0], frac_v)
 
     def peer(k):
         return lax.rem(me + k, half)
@@ -85,6 +80,11 @@
     pl.semaphore_signal(barrier, inc=1, device_id=(mirror, ma), device_id_type=MESH)
     repeat(n_atom - 1, lambda i: pl.semaphore_signal(
         barrier, inc=1, device_id=(shell, atom_at(i + 1)), device_id_type=MESH))
+    c_pts = load(0, pts_h.at[0], pts_v)
+    c_rho = load(1, rho_h, rho_v)
+    c_idx = load(2, idx_h.at[0], idx_v)
+    c_cnt = load(3, cnt_h, cnt_v)
+    c_frac = load(4, frac_h.at[0], frac_v)
     c_green = load(5, green_h, green_v)
 
     def ang_copy(t, to, slot):
@@ -130,12 +130,11 @@
     for copy, low, high in zip(c_ang, bounds, bounds[1:]):
         copy.wait()
         repeat(high - low, lambda i: widen(low + i))
-    repeat(atoms, by_atom)
+    repeat(half, lambda i: by_atom(i * own))
     pl.semaphore_wait(barrier, half + n_atom - 1)
     repeat(half - 1, lambda i: ang_copy(0, far_first(i), me).start())
 
     c_pts.wait()
-    repeat(n_atom - 1, lambda i: pts_copy(atom_at(i + 1), ma).start())
     c_rho.wait()
     c_idx.wait()
     c_cnt.wait()
@@ -175,7 +174,9 @@
     repeat(atoms, build_meta)
     repeat(half - 1, lambda i: meta_copy(far_first(i), me).start())
     for t in range(1, own):
+        repeat(half, lambda i: by_atom(i * own + t))
         repeat(half - 1, lambda i: ang_copy(t, far_first(i), me).start())
+    repeat(n_atom - 1, lambda i: pts_copy(atom_at(i + 1), ma).start())
     rmeta[me] = meta_v[me]
     rpts[ma] = pts_v[...]
     for t in range(own):
@@ -280,11 +281,20 @@
             radial = jnp.dot(table, rows_v[t, b], preferred_element_type=jnp.float32)
             val_v[b, t] = jnp.sum(rang[t, b].astype(jnp.float32) * radial, axis=0, keepdims=True)
 
-        repeat(half - 1, lambda i: evaluate(far_first(i)))
-        evaluate(me)
-    repeat(half - 1, lambda i: val_copy(far_first(i), ma, me, ma).start())
-    for k in range(1, n_atom):
-        repeat(half, lambda i: val_copy(peer(half - 1 - i), atom_at(k), me, ma).start())
+        def finish_batch(b):
+            evaluate(b)
+            if t == own - 1:
+                for k in range(1, n_atom):
+                    val_copy(b, atom_at(k), me, ma).start()
+
+        def finish_far(i):
+            b = far_first(i)
+            finish_batch(b)
+            if t == own - 1:
+                val_copy(b, ma, me, ma).start()
+
+        repeat(half - 1, finish_far)
+        finish_batch(me)
     rval[ma, me] = val_v[me]
 
     def val_batch(group, first, count):

time: 19.2 us -> 19.2 us (level)
  no operation moved by 1% of the time
where the time goes in v7:
time: 19.2 us; the launch traced here: 19.1 us
  Pallas kernels  18.5 us (96%)
  local copies, waits for them, and re-layouts  0.6 us (3%)
    pallas_call x1, Pallas kernels, per_device(): pl.pallas_call(functools.partial(kernel, n_shell, n_atom), out_shape=pltp...  18.5 us
    unnamed x1, local copies, waits for them, and re-layouts  0.6 us

profile of v7, /device:TPU:0, one launch (start us, length us, event | category | flops | bytes accessed | tf_op | source)
XLA Modules:
  0.0 19.1 jit_solution(15429477704621128323)
XLA Ops:
  0.0 18.5 %hartree.1 = f32[8,128]{1,0:T(8,128)S(1)} custom-call(f32[32,128]{1,0:T(8,128)} %bitcast.5, s32[1,8,256]{2,1,0:T(8,128)} %pts_h.1, s32[1,8]{1,0:T(1,128)} %cnt_h.1, s32[1,8,256]{2,1,0:T(8,128)} %idx_h.1, f32[1,8,256]{2,1,0:T(8,128)} %frac_h.1, bf16[1,49,8,256]{3,2,1,0:T(8,128)(2,1)} %bitcast.4, f32[7,128,128]{2,1,0:T(8,128)} %green_h.1), custom_call_target="tpu_custom_call" | custom-call | tf_op jit(solution)/shard_map/hartree/pallas_call | solution.py:384
  18.5 0.6 %copy.9 = f32[1024]{0:T(1024)} copy(f32[1024]{0:T(1024)S(1)} %bitcast.3) | data formatting | bytes 8192

commit v8 on v7

--- a/solution.py
+++ b/solution.py
@@ -60,6 +60,11 @@
         copy.start()
         return copy
 
+    c_pts = load(0, pts_h.at[0], pts_v)
+    c_rho = load(1, rho_h, rho_v)
+    c_idx = load(2, idx_h.at[0], idx_v)
+    c_cnt = load(3, cnt_h, cnt_v)
+    c_frac = load(4, frac_h.at[0], frac_v)
     bounds = [lm * i // PIECES for i in range(PIECES + 1)]
     c_ang = [load(6 + i, ang_h.at[0, pl.ds(low, high - low)], ang_s.at[pl.ds(low, high - low)])
              for i, (low, high) in enumerate(zip(bounds, bounds[1:]))]
@@ -80,11 +85,6 @@
     pl.semaphore_signal(barrier, inc=1, device_id=(mirror, ma), device_id_type=MESH)
     repeat(n_atom - 1, lambda i: pl.semaphore_signal(
         barrier, inc=1, device_id=(shell, atom_at(i + 1)), device_id_type=MESH))
-    c_pts = load(0, pts_h.at[0], pts_v)
-    c_rho = load(1, rho_h, rho_v)
-    c_idx = load(2, idx_h.at[0], idx_v)
-    c_cnt = load(3, cnt_h, cnt_v)
-    c_frac = load(4, frac_h.at[0], frac_v)
     c_green = load(5, green_h, green_v)
 
     def ang_copy(t, to, slot):
@@ -116,23 +116,6 @@
             src_ref=pts_v, dst_ref=rpts.at[slot],
             send_sem=s_pts.at[group], recv_sem=r_pts.at[slot],
             device_id=(shell, group), device_id_type=MESH)
-
-    def widen(m):
-        at = pl.multiple_of(m * atoms, 8) if atoms % 8 == 0 else m * atoms
-        for h in range(halves):
-            ang_f[h, pl.ds(at, atoms), :] = ang_s[m, :, h * LANES:(h + 1) * LANES].astype(jnp.float32)
-
-    def by_atom(a):
-        for h in range(halves):
-            ang_v[a, :, h * LANES:(h + 1) * LANES] = ang_f[
-                h, pl.ds(a, body_rows, stride=atoms), :].astype(jnp.bfloat16)
-
-    for copy, low, high in zip(c_ang, bounds, bounds[1:]):
-        copy.wait()
-        repeat(high - low, lambda i: widen(low + i))
-    repeat(half, lambda i: by_atom(i * own))
-    pl.semaphore_wait(barrier, half + n_atom - 1)
-    repeat(half - 1, lambda i: ang_copy(0, far_first(i), me).start())
 
     c_pts.wait()
     c_rho.wait()
@@ -166,15 +149,34 @@
         meta_v[to, t, 0:1, :] = jnp.sum(jnp.where(here, found, 0.0), axis=0, keepdims=True)
         meta_v[to, t, 1:2, :] = live_v[pl.ds(a, 1), :]
         meta_v[to, t, 2:3, :] = frac_v[pl.ds(a, 1), :]
+    repeat(atoms, build_meta)
+
+    def widen(m):
+        at = pl.multiple_of(m * atoms, 8) if atoms % 8 == 0 else m * atoms
+        for h in range(halves):
+            ang_f[h, pl.ds(at, atoms), :] = ang_s[m, :, h * LANES:(h + 1) * LANES].astype(jnp.float32)
+
+    def by_atom(a):
+        for h in range(halves):
+            ang_v[a, :, h * LANES:(h + 1) * LANES] = ang_f[
+                h, pl.ds(a, body_rows, stride=atoms), :].astype(jnp.bfloat16)
+
+    for copy, low, high in zip(c_ang, bounds, bounds[1:]):
+        copy.wait()
+        repeat(high - low, lambda i: widen(low + i))
+    repeat(atoms, by_atom)
+
+    def last_rows(a):
+        to, t = a // own, a % own
         for j in range(rest):
             for h in range(halves):
                 meta_v[to, t, 3 + j:4 + j, h * LANES:(h + 1) * LANES] = ang_f[
                     h, pl.ds((body_rows + j) * atoms + a, 1), :]
 
-    repeat(atoms, build_meta)
+    repeat(atoms, last_rows)
+    pl.semaphore_wait(barrier, half + n_atom - 1)
     repeat(half - 1, lambda i: meta_copy(far_first(i), me).start())
-    for t in range(1, own):
-        repeat(half, lambda i: by_atom(i * own + t))
+    for t in range(own):
         repeat(half - 1, lambda i: ang_copy(t, far_first(i), me).start())
     repeat(n_atom - 1, lambda i: pts_copy(atom_at(i + 1), ma).start())
     rmeta[me] = meta_v[me]
@@ -206,10 +208,10 @@
         return lax.dot_general(weighted, rows_v[t, s], NT, preferred_element_type=jnp.float32)
 
     def take_batch(t, i):
-        s = peer(i + 1)
+        s = i + jnp.where(i >= me, 1, 0)
         if t == 0:
             meta_copy(me, s).wait_recv()
-            make_rows(t, s)
+        make_rows(t, s)
         ang_copy(t, me, s).wait_recv()
         return add_batch(t, s)
 
@@ -227,16 +229,6 @@
         mom_h, mom_l = split2(mom)
         both = solve(jnp.concatenate([mom_h.astype(jnp.float32), mom_l.astype(jnp.float32)], axis=0))
         return both[0:lmp] + both[lmp:]
-
-    for t in range(own):
-        make_rows(t, me)
-    partial = [add_batch(t, me) for t in range(own)]
-    for t in range(own):
-        partial[t] = accumulate(half - 1, functools.partial(take_batch, t), partial[t])
-        mom_v[t] = partial[t].astype(jnp.bfloat16)
-        mom_copy(t).start()
-        if t + 1 < own:
-            repeat(half - 1, lambda i: make_rows(t + 1, peer(i + 1)))
 
     share = out_ref.shape[0]
     cells = LANES // FINE
@@ -259,10 +251,49 @@
 
         repeat(atoms, mark)
 
+    for t in range(own):
+        make_rows(t, me)
+    partial = [add_batch(t, me) for t in range(own)]
+    if half <= 16:
+        for i in range(half - 2):
+            for t in range(own):
+                partial[t] = partial[t] + take_batch(t, i)
+    else:
+        partial = list(lax.fori_loop(
+            0, half - 2, lambda i, c: tuple(c[t] + take_batch(t, i) for t in range(own)), tuple(partial)))
+    for t in range(own):
+        partial[t] = partial[t] + take_batch(t, half - 2)
+        mom_v[t] = partial[t].astype(jnp.bfloat16)
+        mom_copy(t).start()
+
     for k in range(n_atom):
         find_spots(k)
 
     solved = [solve_own(partial[t]) for t in range(own)]
+
+    for t in range(own):
+        mom_copy(t).wait_recv()
+        table = (solved[t] + solve(rmom[t].astype(jnp.float32))).astype(jnp.bfloat16)
+
+        def evaluate(b):
+            radial = jnp.dot(table, rows_v[t, b], preferred_element_type=jnp.float32)
+            val_v[b, t] = jnp.sum(rang[t, b].astype(jnp.float32) * radial, axis=0, keepdims=True)
+
+        def finish_batch(b):
+            evaluate(b)
+            if t == own - 1:
+                for k in range(1, n_atom):
+                    val_copy(b, atom_at(k), me, ma).start()
+
+        def finish_far(i):
+            b = far_first(i)
+            finish_batch(b)
+            if t == own - 1:
+                val_copy(b, ma, me, ma).start()
+
+        repeat(half - 1, finish_far)
+        finish_batch(me)
+    rval[ma, me] = val_v[me]
 
     def sent(i):
         to = peer(i + 1)
@@ -272,36 +303,18 @@
 
     repeat(half - 1, sent)
     repeat(n_atom - 1, lambda i: pts_copy(atom_at(i + 1), ma).wait_send())
-
-    for t in range(own):
-        mom_copy(t).wait_recv()
-        table = (solved[t] + solve(rmom[t].astype(jnp.float32))).astype(jnp.bfloat16)
-
-        def evaluate(b):
-            radial = jnp.dot(table, rows_v[t, b], preferred_element_type=jnp.float32)
-            val_v[b, t] = jnp.sum(rang[t, b].astype(jnp.float32) * radial, axis=0, keepdims=True)
-
-        def finish_batch(b):
-            evaluate(b)
-            if t == own - 1:
-                for k in range(1, n_atom):
-                    val_copy(b, atom_at(k), me, ma).start()
-
-        def finish_far(i):
-            b = far_first(i)
-            finish_batch(b)
-            if t == own - 1:
-                val_copy(b, ma, me, ma).start()
-
-        repeat(half - 1, finish_far)
-        finish_batch(me)
-    rval[ma, me] = val_v[me]
+    for t in range(own):
+        mom_copy(t).wait_send()
 
     def val_batch(group, first, count):
         return pltpu.make_async_remote_copy(
             src_ref=val_v.at[pl.ds(first, count)], dst_ref=rval.at[group, pl.ds(first, count)],
             send_sem=s_val.at[group], recv_sem=r_val.at[group],
             device_id=(mirror, ma), device_id_type=MESH)
+
+    val_batch(ma, 0, half - 1).wait_send()
+    for k in range(1, n_atom):
+        val_batch(atom_at(k), 0, half).wait_send()
 
     spot_ids = lax.broadcasted_iota(jnp.int32, (cells * share, slots), 0)
 
@@ -328,12 +341,6 @@
     terms = terms[0:cells * share] + terms[cells * share:]
     out_ref[...] = jnp.concatenate(
         [terms[c * share:(c + 1) * share] for c in range(cells)], axis=1)
-
-    val_batch(ma, 0, half - 1).wait_send()
-    for k in range(1, n_atom):
-        val_batch(atom_at(k), 0, half).wait_send()
-    for t in range(own):
-        mom_copy(t).wait_send()
 
 
 def solution(mesh):

time: 19.2 us -> 19.8 us (1.031)
  Pallas kernels: 18.5 us -> 19 us
    pallas_call x1, Pallas kernels: 18.5 us -> 19 us  [per_device(): pl.pallas_call(functools.partial(kernel, n_shell, n_atom), out_shape=pltp...]
where the time goes in v8:
time: 19.8 us; the launch traced here: 19.6 us
  Pallas kernels  19 us (96%)
  local copies, waits for them, and re-layouts  0.6 us (3%)
    pallas_call x1, Pallas kernels, per_device(): pl.pallas_call(functools.partial(kernel, n_shell, n_atom), out_shape=pltp...  19 us
    unnamed x1, local copies, waits for them, and re-layouts  0.6 us

profile of v8, /device:TPU:0, one launch (start us, length us, event | category | flops | bytes accessed | tf_op | source)
XLA Modules:
  0.0 19.6 jit_solution(6315562891132204385)
XLA Ops:
  0.0 19.0 %hartree.1 = f32[8,128]{1,0:T(8,128)S(1)} custom-call(f32[32,128]{1,0:T(8,128)} %bitcast.5, s32[1,8,256]{2,1,0:T(8,128)} %pts_h.1, s32[1,8]{1,0:T(1,128)} %cnt_h.1, s32[1,8,256]{2,1,0:T(8,128)} %idx_h.1, f32[1,8,256]{2,1,0:T(8,128)} %frac_h.1, bf16[1,49,8,256]{3,2,1,0:T(8,128)(2,1)} %bitcast.4, f32[7,128,128]{2,1,0:T(8,128)} %green_h.1), custom_call_target="tpu_custom_call" | custom-call | tf_op jit(solution)/shard_map/hartree/pallas_call | solution.py:391
  19.0 0.6 %copy.9 = f32[1024]{0:T(1024)} copy(f32[1024]{0:T(1024)S(1)} %bitcast.3) | data formatting | bytes 8192

commit v9 on v7

--- a/solution.py
+++ b/solution.py
@@ -228,16 +228,6 @@
         both = solve(jnp.concatenate([mom_h.astype(jnp.float32), mom_l.astype(jnp.float32)], axis=0))
         return both[0:lmp] + both[lmp:]
 
-    for t in range(own):
-        make_rows(t, me)
-    partial = [add_batch(t, me) for t in range(own)]
-    for t in range(own):
-        partial[t] = accumulate(half - 1, functools.partial(take_batch, t), partial[t])
-        mom_v[t] = partial[t].astype(jnp.bfloat16)
-        mom_copy(t).start()
-        if t + 1 < own:
-            repeat(half - 1, lambda i: make_rows(t + 1, peer(i + 1)))
-
     share = out_ref.shape[0]
     cells = LANES // FINE
     cell_ids = lax.broadcasted_iota(jnp.int32, (FINE, slots), 0)
@@ -259,10 +249,44 @@
 
         repeat(atoms, mark)
 
+    for t in range(own):
+        make_rows(t, me)
+    partial = [add_batch(t, me) for t in range(own)]
+    for t in range(own):
+        partial[t] = accumulate(half - 1, functools.partial(take_batch, t), partial[t])
+        mom_v[t] = partial[t].astype(jnp.bfloat16)
+        mom_copy(t).start()
+        if t + 1 < own:
+            repeat(half - 1, lambda i: make_rows(t + 1, peer(i + 1)))
+
     for k in range(n_atom):
         find_spots(k)
 
     solved = [solve_own(partial[t]) for t in range(own)]
+
+    for t in range(own):
+        mom_copy(t).wait_recv()
+        table = (solved[t] + solve(rmom[t].astype(jnp.float32))).astype(jnp.bfloat16)
+
+        def evaluate(b):
+            radial = jnp.dot(table, rows_v[t, b], preferred_element_type=jnp.float32)
+            val_v[b, t] = jnp.sum(rang[t, b].astype(jnp.float32) * radial, axis=0, keepdims=True)
+
+        def finish_batch(b):
+            evaluate(b)
+            if t == own - 1:
+                for k in range(1, n_atom):
+                    val_copy(b, atom_at(k), me, ma).start()
+
+        def finish_far(i):
+            b = far_first(i)
+            finish_batch(b)
+            if t == own - 1:
+                val_copy(b, ma, me, ma).start()
+
+        repeat(half - 1, finish_far)
+        finish_batch(me)
+    rval[ma, me] = val_v[me]
 
     def sent(i):
         to = peer(i + 1)
@@ -272,36 +296,18 @@
 
     repeat(half - 1, sent)
     repeat(n_atom - 1, lambda i: pts_copy(atom_at(i + 1), ma).wait_send())
-
     for t in range(own):
-        mom_copy(t).wait_recv()
-        table = (solved[t] + solve(rmom[t].astype(jnp.float32))).astype(jnp.bfloat16)
-
-        def evaluate(b):
-            radial = jnp.dot(table, rows_v[t, b], preferred_element_type=jnp.float32)
-            val_v[b, t] = jnp.sum(rang[t, b].astype(jnp.float32) * radial, axis=0, keepdims=True)
-
-        def finish_batch(b):
-            evaluate(b)
-            if t == own - 1:
-                for k in range(1, n_atom):
-                    val_copy(b, atom_at(k), me, ma).start()
-
-        def finish_far(i):
-            b = far_first(i)
-            finish_batch(b)
-            if t == own - 1:
-                val_copy(b, ma, me, ma).start()
-
-        repeat(half - 1, finish_far)
-        finish_batch(me)
-    rval[ma, me] = val_v[me]
+        mom_copy(t).wait_send()
 
     def val_batch(group, first, count):
         return pltpu.make_async_remote_copy(
             src_ref=val_v.at[pl.ds(first, count)], dst_ref=rval.at[group, pl.ds(first, count)],
             send_sem=s_val.at[group], recv_sem=r_val.at[group],
             device_id=(mirror, ma), device_id_type=MESH)
+
+    val_batch(ma, 0, half - 1).wait_send()
+    for k in range(1, n_atom):
+        val_batch(atom_at(k), 0, half).wait_send()
 
     spot_ids = lax.broadcasted_iota(jnp.int32, (cells * share, slots), 0)
 
@@ -328,12 +334,6 @@
     terms = terms[0:cells * share] + terms[cells * share:]
     out_ref[...] = jnp.concatenate(
         [terms[c * share:(c + 1) * share] for c in range(cells)], axis=1)
-
-    val_batch(ma, 0, half - 1).wait_send()
-    for k in range(1, n_atom):
-        val_batch(atom_at(k), 0, half).wait_send()
-    for t in range(own):
-        mom_copy(t).wait_send()
 
 
 def solution(mesh):

time: 19.2 us -> 19.2 us (level)
  no operation moved by 1% of the time
where the time goes in v9:
time: 19.2 us; the launch traced here: 19.1 us
  Pallas kernels  18.5 us (96%)
  local copies, waits for them, and re-layouts  0.6 us (3%)
    pallas_call x1, Pallas kernels, per_device(): pl.pallas_call(functools.partial(kernel, n_shell, n_atom), out_shape=pltp...  18.5 us
    unnamed x1, local copies, waits for them, and re-layouts  0.6 us

profile of v9, /device:TPU:0, one launch (start us, length us, event | category | flops | bytes accessed | tf_op | source)
XLA Modules:
  0.0 19.1 jit_solution(11052026569506181902)
XLA Ops:
  0.0 18.5 %hartree.1 = f32[8,128]{1,0:T(8,128)S(1)} custom-call(f32[32,128]{1,0:T(8,128)} %bitcast.5, s32[1,8,256]{2,1,0:T(8,128)} %pts_h.1, s32[1,8]{1,0:T(1,128)} %cnt_h.1, s32[1,8,256]{2,1,0:T(8,128)} %idx_h.1, f32[1,8,256]{2,1,0:T(8,128)} %frac_h.1, bf16[1,49,8,256]{3,2,1,0:T(8,128)(2,1)} %bitcast.4, f32[7,128,128]{2,1,0:T(8,128)} %green_h.1), custom_call_target="tpu_custom_call" | custom-call | tf_op jit(solution)/shard_map/hartree/pallas_call | solution.py:384
  18.5 0.6 %copy.9 = f32[1024]{0:T(1024)} copy(f32[1024]{0:T(1024)S(1)} %bitcast.3) | data formatting | bytes 8192
